TPU v7x, 32 devices: a whole 2x2x4 slice. The times are simulated.
32 devices in a mesh: group: 4 (over y, core), inner: 8 (over z, x).
Axes of the slice: x: 2, y: 2, z: 4, core: 2. Of those that a mesh axis runs over, the one named last changes fastest.
Arguments:
- pair_rows: bfloat16 [512, 2048], P(('group', 'inner')), may hold values from -6 to 6
- group_ids: int32 [512, 1], P(('group', 'inner')), may hold values from 0 to 3; in each aligned block of 16 rows (0 to 15, 16 to 31, ...) at most 8 rows name the same one
- local_ids: int32 [512, 1], P(('group', 'inner')), may hold values from 0 to 1
- route_weight: float32 [512], P(('group', 'inner')), may hold values from 0.3 to 1
- w_up: bfloat16 [8, 2048, 8192], P('group', None, 'inner'), may hold values from -0.125 to 0.125
- w_down: bfloat16 [8, 8192, 2048], P('group', 'inner'), may hold values from -0.0625 to 0.0625
Outputs:
- mixed: bfloat16 [512, 2048], P(('group', 'inner'))
Inputs may be any that keep to these rules, and one draw needn't show every extreme that they name: `group_ids`: among the rows of one device no value is named more than 8 times, a bound that some block reaches.
All inputs are finite; a program needn't handle non-finite values.
Results may differ from a plain program's by a relative error of at most 0.02.
Values may be sent and summed in bfloat16 or wider, within the bound.
No kernel may reach another device: no remote copies, remote signals or barrier semaphores. Data moves between devices by JAX's collectives and lax.ppermute only.
A program may use at most 64 MiB of HBM per device.

v0:
```python
import functools

import jax
import jax.numpy as jnp
from jax import lax
from jax.experimental import pallas as pl
from jax.experimental.pallas import tpu as pltpu
from jax.sharding import PartitionSpec as P

LANES = 128
STACK_FLOPS = 6 * 10**9
PACK_FLOPS = 15 * 10**8
MIB = 2**20
BF16 = jnp.bfloat16
F32 = jnp.float32
VMEM_SPEC = pl.BlockSpec(memory_space=pltpu.VMEM)
ANY_SPEC = pl.BlockSpec(memory_space=pl.ANY)
HBM_SPEC = pl.BlockSpec(memory_space=pltpu.HBM)


def call(kernel, name, outs, args, limit=4, scratch=(), flops=0, moved=0, specs=None):
    shapes = [jax.ShapeDtypeStruct(shape, dtype) for shape, dtype in outs]
    return pl.pallas_call(
        kernel,
        out_shape=shapes,
        in_specs=specs or [VMEM_SPEC] * len(args),
        out_specs=[VMEM_SPEC] * len(shapes),
        scratch_shapes=list(scratch),
        compiler_params=pltpu.CompilerParams(vmem_limit_bytes=limit * MIB),
        cost_estimate=pl.CostEstimate(flops=flops, bytes_accessed=moved, transcendentals=0),
        name=name,
    )(*args)


def column(row_ref, count):
    across = lax.broadcasted_iota(jnp.int32, (count, count), 1)
    down = lax.broadcasted_iota(jnp.int32, (count, count), 0)
    spread = jnp.broadcast_to(row_ref[...], (count, count))
    return jnp.sum(jnp.where(across == down, spread, jnp.zeros_like(spread)), axis=1, keepdims=True)


def tag_kernel(capacity, experts, rows_ref, expert_ref, out_ref):
    count, width = rows_ref.shape
    across = lax.broadcasted_iota(jnp.int32, (count, count), 1)
    down = lax.broadcasted_iota(jnp.int32, (count, count), 0)
    lane = lax.broadcasted_iota(jnp.int32, (count, LANES), 1)
    group_across = expert_ref[...] // experts
    expert_down = column(expert_ref, count)
    group_down = expert_down // experts
    before = (jnp.broadcast_to(group_across, (count, count)) == group_down) & (across < down)
    slot = group_down * capacity + jnp.sum(jnp.where(before, 1, 0), axis=1, keepdims=True)
    local_down = expert_down % experts
    tags = jnp.where(lane == 0, slot, jnp.where(lane == 1, local_down + 1, 0))
    out_ref[:, :width] = rows_ref[...]
    out_ref[:, width:] = tags.astype(F32).astype(BF16)


def stack_kernel(owners, *refs):
    out_refs = refs[owners:]
    count, full = refs[0].shape
    for which in range(owners):
        here = slice(which * count, (which + 1) * count)
        start = 0
        for part, out_ref in enumerate(out_refs):
            width = out_ref.shape[1] - (LANES if part == 0 else 0)
            out_ref[here, :width] = refs[which][:, start : start + width]
            start += width
        out_refs[0][here, out_refs[0].shape[1] - LANES :] = refs[which][:, full - LANES :]


def pack_kernel(capacity, owners, blocks, width, first, *refs):
    if first:
        own_ref, other_ref, onehot_ref = refs[blocks + 1 :]
    else:
        onehot_ref, own_ref, other_ref = refs[blocks:]
    block = owners * capacity
    rows = refs[0].shape[0]
    count = rows // owners
    if first:
        me = lax.axis_index("group")
        col = lax.broadcasted_iota(jnp.int32, (rows, 2 * block), 1)
        owner_col = (col % block) // capacity
        owner_row = lax.broadcasted_iota(jnp.int32, (rows, 2 * block), 0) // count
        wanted = (me ^ (col // block)) * capacity + col % capacity
    for which in range(blocks):
        ref = refs[which]
        here = slice(which * block, (which + 1) * block)
        if first:
            tags = ref[:, width:]
            slot = tags.astype(F32)[:, 0:1].astype(jnp.int32)
            onehot = ((slot == wanted) & (owner_col == owner_row)).astype(F32).astype(BF16)
            onehot_ref[which * rows : (which + 1) * rows, :] = onehot
        else:
            onehot = onehot_ref[which * rows : (which + 1) * rows, :]

        def packed(value):
            return lax.dot_general(
                onehot, value, (((0,), (0,)), ((), ())), preferred_element_type=F32
            ).astype(BF16)

        value = packed(ref[:, :width])
        own_ref[here, :width] = value[:block]
        other_ref[here, :width] = value[block:]
        if first:
            value = packed(tags)
            own_ref[here, width:] = value[:block]
            other_ref[here, width:] = value[block:]


def load_kernel(after_ref, weight_ref, held_ref, token_ref, sem):
    copies = [
        pltpu.make_async_copy(weight_ref.at[e], held_ref.at[e], sem.at[e])
        for e in range(weight_ref.shape[0])
    ]
    for copy in copies:
        copy.start()
    token_ref[...] = jnp.zeros_like(token_ref)
    for copy in copies:
        copy.wait()


def up_product(own_ref, other_ref, up_ref, expert, start, width, cols):
    rows = jnp.concatenate([own_ref[:, :width], other_ref[:, :width]], axis=0)
    return jnp.dot(rows, up_ref[expert, start : start + width, cols], preferred_element_type=F32)


def up_first_kernel(step, width, own_ref, other_ref, up_ref, acc_ref):
    experts, _, units = up_ref.shape
    for expert in range(experts):
        for at in range(0, units, step):
            acc_ref[:, expert * units + at : expert * units + at + step] = up_product(
                own_ref, other_ref, up_ref, expert, 0, width, slice(at, at + step)
            )


def up_last_kernel(step, start, width, own_tag, other_tag, own_ref, other_ref, up_ref, acc_ref, hidden_ref):
    experts, _, units = up_ref.shape
    full = own_tag.shape[1]
    chosen = jnp.concatenate(
        [own_tag[:, full - LANES :].astype(F32)[:, 1:2], other_tag[:, full - LANES :].astype(F32)[:, 1:2]],
        axis=0,
    )
    for expert in range(experts):
        mine = chosen == float(expert + 1)
        for at in range(0, units, step):
            cols = slice(expert * units + at, expert * units + at + step)
            value = acc_ref[:, cols] + up_product(
                own_ref, other_ref, up_ref, expert, start, width, slice(at, at + step)
            )
            value = jnp.where(mine, value / (1.0 + jnp.exp(-value)), 0.0)
            hidden_ref[:, cols] = value.astype(BF16)


def down_kernel(step, start, width, hidden_ref, down_ref, own_ref, other_ref):
    experts, units, _ = down_ref.shape
    half = own_ref.shape[0]
    for at in range(0, width, step):
        total = None
        for expert in range(experts):
            term = jnp.dot(
                hidden_ref[:, expert * units : (expert + 1) * units],
                down_ref[expert, :, start + at : start + at + step],
                preferred_element_type=F32,
            )
            total = term if total is None else total + term
        total = total.astype(BF16)
        own_ref[:, at : at + step] = total[:half]
        other_ref[:, at : at + step] = total[half:]


def dense_block(which, block, rows, onehot_ref, own_ref, other_ref):
    here = slice(which * block, (which + 1) * block)
    slots = jnp.concatenate([own_ref[here, :], other_ref[here, :]], axis=0)
    onehot = onehot_ref[which * rows : (which + 1) * rows, :]
    return jnp.dot(onehot, slots, preferred_element_type=F32).astype(BF16)


def unpack_kernel(onehot_ref, own_ref, other_ref, *out_refs):
    block = onehot_ref.shape[1] // 2
    rows = out_refs[0].shape[0]
    for which, out_ref in enumerate(out_refs):
        here = slice(which * block, (which + 1) * block)
        slots = jnp.concatenate([own_ref[here, :], other_ref[here, :]], axis=0)
        onehot = onehot_ref[which * rows : (which + 1) * rows, :]
        out_ref[...] = jnp.dot(onehot, slots, preferred_element_type=F32).astype(BF16)


def add_kernel(chunks, terms, *refs):
    out_refs = refs[chunks * terms :]
    count = out_refs[0].shape[0]
    start = 0
    for chunk in range(chunks):
        blocks = refs[chunk * terms : (chunk + 1) * terms]
        total = blocks[0][...].astype(F32)
        for ref in blocks[1:]:
            total += ref[...].astype(F32)
        total = total.astype(BF16)
        width = total.shape[1]
        for piece, out_ref in enumerate(out_refs):
            out_ref[:, start : start + width] = total[piece * count : (piece + 1) * count]
        start += width


def finish_kernel(weight_ref, *refs):
    out_ref = refs[-1]
    weight = column(weight_ref, out_ref.shape[0])
    total = refs[0][...].astype(F32)
    for ref in refs[1:-1]:
        total += ref[...].astype(F32)
    out_ref[...] = (total.astype(BF16).astype(F32) * weight).astype(BF16)


def body(pair_rows, group_ids, local_ids, route_weight, w_up, w_down):
    groups = lax.axis_size("group")
    inner = lax.axis_size("inner")
    near, turns = 2, groups // 2
    far = inner // near
    count, model = pair_rows.shape
    experts, _, units = w_up.shape
    capacity = 2 * count // groups
    block = far * capacity
    blocks = turns * near
    rows = far * count
    half = blocks * block
    widths = [model // 2, model // 2]
    chunks = len(widths)
    starts = [sum(widths[:i]) for i in range(chunks)]
    step = min(256, units)


    mixed = far == blocks

    def exchange(value, wide, index):
        pairs = []
        for g in range(groups):
            for i in range(inner):
                if wide != (mixed and g % 2 == 1):
                    to = (g ^ 2 * (index // near)) * inner + (i ^ index % near)
                else:
                    to = g * inner + (i ^ near * index)
                pairs.append((g * inner + i, to))
        return lax.ppermute(value, ("group", "inner"), pairs)

    def along_group(value, flip):
        return lax.ppermute(value, "group", [(g, g ^ flip) for g in range(groups)])

    full = model + LANES
    named = group_ids * experts + local_ids
    (tagged,) = call(
        functools.partial(tag_kernel, capacity, experts),
        "tag_rows",
        [((count, full), BF16)],
        [pair_rows, named.reshape(1, count)],
    )

    pieces = [exchange(tagged, False, s) for s in range(far - 1, 0, -1)] + [tagged]
    pieces.reverse()
    parts = call(
        functools.partial(stack_kernel, far),
        "stack_rows",
        [((rows, w + (LANES if i == 0 else 0)), BF16) for i, w in enumerate(widths)],
        pieces,
        flops=STACK_FLOPS,
    )

    onehot = None
    slots = []
    for chunk, width in enumerate(widths):
        first = chunk == 0
        arrived = [parts[chunk]] + [exchange(parts[chunk], True, s) for s in range(1, blocks)]
        if first:
            down_held, down_token = call(
                load_kernel,
                "load_down",
                [(w_down.shape, BF16), ((8, LANES), F32)],
                [arrived[-1], w_down],
                specs=[ANY_SPEC, HBM_SPEC],
                scratch=[pltpu.SemaphoreType.DMA((experts,))],
                moved=4 * w_down.size,
                limit=38,
            )
        outs = [((half, width + LANES * first), BF16)] * 2
        if first:
            outs.append(((blocks * rows, 2 * block), BF16))
        packed = call(
            functools.partial(pack_kernel, capacity, far, blocks, width, first),
            f"pack_{chunk}",
            outs,
            [*arrived, down_token] if first else [*arrived, onehot],
            flops=PACK_FLOPS,
        )
        if first:
            onehot = packed[2]
        slots.append((packed[0], along_group(packed[1], 1)))

    work = 2 * 2 * half * experts * units
    acc = call(
        functools.partial(up_first_kernel, step, widths[0]),
        "up_first",
        [((2 * half, experts * units), F32)],
        [*slots[0], w_up],
        limit=8,
        flops=work * widths[0],
    )[0]
    (hidden,) = call(
        functools.partial(up_last_kernel, step, starts[1], widths[1]),
        "up_last",
        [((2 * half, experts * units), BF16)],
        [*slots[0], *slots[1], w_up, acc],
        limit=8,
        flops=work * widths[1],
    )

    terms = [None] * chunks
    for chunk in reversed(range(chunks)):
        width = widths[chunk]
        own, other = call(
            functools.partial(down_kernel, min(256, width), starts[chunk], width),
            f"down_{chunk}",
            [((half, width), BF16)] * 2,
            [hidden, down_held],
            limit=8,
            flops=work * width,
        )
        dense = call(
            unpack_kernel,
            "unpack_slots",
            [((rows, width), BF16)] * blocks,
            [onehot, own, along_group(other, 1)],
        )
        terms[chunk] = [dense[0]] + [exchange(dense[s], True, s) for s in range(blocks - 1, 0, -1)]
    sums = call(
        functools.partial(add_kernel, chunks, blocks),
        "add_plane",
        [((count, model), BF16)] * far,
        sum(terms, []),
    )
    parts = [sums[0]] + [exchange(sums[s], False, s) for s in range(far - 1, 0, -1)]
    return call(
        finish_kernel, "finish", [((count, model), BF16)], [route_weight.reshape(1, count), *parts]
    )[0]


def solution(mesh):
    placed = (
        P(("group", "inner"), None),
        P(("group", "inner"), None),
        P(("group", "inner"), None),
        P(("group", "inner")),
        P("group", None, "inner"),
        P("group", "inner", None),
    )
    return jax.shard_map(
        body, mesh=mesh, in_specs=placed, out_specs=P(("group", "inner"), None), check_vma=False
    )
```

profile of v0, /device:TPU:0, one launch (start us, length us, event | category | flops | bytes accessed | tf_op | source)
XLA Modules:
  0.0 52.5 jit_solution(11058039388111427308)
XLA Ops:
  0.0 0.7 %add_bitcast_fusion.expert_ref = s32[1,16]{1,0:T(1,128)S(1)} fusion(s32[16,1]{0,1:T(1,128)} %param.8, s32[16,1]{0,1:T(1,128)} %param.7), kind=kLoop, calls=%fused_computation | loop fusion | flops 32 | bytes 192 | tf_op jit(solution)/shard_map/reshape | solution.py:253
  0.7 0.0 copy-start
  0.7 0.8 %copy-done = bf16[16,2048]{1,0:T(8,128)(2,1)S(1)} copy-done((bf16[16,2048]{1,0:T(8,128)(2,1)S(1)}, bf16[16,2048]{1,0:T(8,128)(2,1)}, u32[]{:S(2)}) %copy-start) | copy-done | bytes 65560
  1.5 0.2 tag_rows.1.refs_0_
  1.7 5.1 %collective-permute-start.2 = (bf16[16,2176]{1,0:T(8,128)(2,1)S(1)}, bf16[16,2176]{1,0:T(8,128)(2,1)S(1)}, u32[]{:S(2)}, u32[]{:S(2)}) collective-permute-start(bf16[16,2176]{1,0:T(8,128)(2,1)S(1)} %tag_rows.1.refs_0_), channel_id=1, source_target_pairs={{0,6},{1,7},{2,4},{3,5},{4,2},{5,3},{6,0},{7,1},{8,25},{9,24},{10,... | collective-permute-start | bytes 208904 | tf_op jit(solution)/shard_map/ppermute | solution.py:242
  6.8 0.0 collective-permute-start.1
  6.8 0.6 %collective-permute-start = (bf16[16,2176]{1,0:T(8,128)(2,1)S(1)}, bf16[16,2176]{1,0:T(8,128)(2,1)S(1)}, u32[]{:S(2)}, u32[]{:S(2)}) collective-permute-start(bf16[16,2176]{1,0:T(8,128)(2,1)S(1)} %tag_rows.1.refs_0_), channel_id=1, source_target_pairs={{0,2},{1,3},{2,0},{3,1},{4,6},{5,7},{6,4},{7,5},{8,9},{9,8},{10,11... | collective-permute-start | bytes 208904 | tf_op jit(solution)/shard_map/ppermute | solution.py:242
  7.4 1.8 %collective-permute-done.2.refs_3_ = bf16[16,2176]{1,0:T(8,128)(2,1)S(1)} collective-permute-done((bf16[16,2176]{1,0:T(8,128)(2,1)S(1)}, bf16[16,2176]{1,0:T(8,128)(2,1)S(1)}, u32[]{:S(2)}, u32[]{:S(2)}) %collective-permute-start.2) | collective-permute-done | bytes 69664 | tf_op jit(solution)/shard_map/ppermute | solution.py:242
  9.2 2.8 %collective-permute-done.1.refs_2_ = bf16[16,2176]{1,0:T(8,128)(2,1)S(1)} collective-permute-done((bf16[16,2176]{1,0:T(8,128)(2,1)S(1)}, bf16[16,2176]{1,0:T(8,128)(2,1)S(1)}, u32[]{:S(2)}, u32[]{:S(2)}) %collective-permute-start.1) | collective-permute-done | bytes 69664 | tf_op jit(solution)/shard_map/ppermute | solution.py:242
  12.0 0.0 collective-permute-done.refs_1_
  12.0 4.3 %collective-permute-start.5 = (bf16[64,1152]{1,0:T(8,128)(2,1)S(1)}, bf16[64,1152]{1,0:T(8,128)(2,1)S(1)}, u32[]{:S(2)}, u32[]{:S(2)}) collective-permute-start(bf16[64,1152]{1,0:T(8,128)(2,1)S(1)} %get-tuple-element.30.refs_0_), channel_id=1, source_target_pairs={{0,17},{1,16},{2,19},{3,18},{4,21},{5,20},{6,23},{7,22},{8,14},{9,... | collective-permute-start | bytes 442376 | tf_op jit(solution)/shard_map/ppermute | solution.py:242
  16.3 0.0 collective-permute-start.4
  16.3 0.6 %collective-permute-start.3 = (bf16[64,1152]{1,0:T(8,128)(2,1)S(1)}, bf16[64,1152]{1,0:T(8,128)(2,1)S(1)}, u32[]{:S(2)}, u32[]{:S(2)}) collective-permute-start(bf16[64,1152]{1,0:T(8,128)(2,1)S(1)} %get-tuple-element.30.refs_0_), channel_id=1, source_target_pairs={{0,1},{1,0},{2,3},{3,2},{4,5},{5,4},{6,7},{7,6},{8,10},{9,11},{10,... | collective-permute-start | bytes 442376 | tf_op jit(solution)/shard_map/ppermute | solution.py:242
  16.9 2.8 %collective-permute-start.9 = (bf16[64,1024]{1,0:T(8,128)(2,1)S(1)}, bf16[64,1024]{1,0:T(8,128)(2,1)S(1)}, u32[]{:S(2)}, u32[]{:S(2)}) collective-permute-start(bf16[64,1024]{1,0:T(8,128)(2,1)S(1)} %get-tuple-element.35.refs_0_), channel_id=1, source_target_pairs={{0,17},{1,16},{2,19},{3,18},{4,21},{5,20},{6,23},{7,22},{8,14},{9,... | collective-permute-start | bytes 393224 | tf_op jit(solution)/shard_map/ppermute | solution.py:242
  19.8 0.0 collective-permute-start.8
  19.8 0.0 collective-permute-done.5.after_ref.refs_3_
  19.8 0.6 %collective-permute-start.7 = (bf16[64,1024]{1,0:T(8,128)(2,1)S(1)}, bf16[64,1024]{1,0:T(8,128)(2,1)S(1)}, u32[]{:S(2)}, u32[]{:S(2)}) collective-permute-start(bf16[64,1024]{1,0:T(8,128)(2,1)S(1)} %get-tuple-element.35.refs_0_), channel_id=1, source_target_pairs={{0,1},{1,0},{2,3},{3,2},{4,5},{5,4},{6,7},{7,6},{8,10},{9,11},{10,... | collective-permute-start | bytes 393224 | tf_op jit(solution)/shard_map/ppermute | solution.py:242
  20.4 3.5 %load_down.1 = (bf16[2,1024,2048]{2,1,0:T(8,128)(2,1)S(1)}, f32[8,128]{1,0:T(8,128)S(1)}) custom-call(bf16[64,1152]{1,0:T(8,128)(2,1)S(1)} %collective-permute-done.5.after_ref.refs_3_, bf16[2,1024,2048]{2,1,0:T(8,128)(2,1)} %weight_ref.1), custom_call_target="tpu_custom_call" | custom-call | bytes 16777216 | tf_op jit(solution)/shard_map/load_down/pallas_call | solution.py:23
  23.9 0.0 collective-permute-done.4.refs_2_
  23.9 0.0 collective-permute-done.3.refs_1_
  23.9 0.0 slice-start.1
  24.0 0.4 pack_0.1
  24.4 0.1 collective-permute-start.6
  24.5 0.0 collective-permute-done.9.refs_3_
  24.5 1.2 %collective-permute-done.8.refs_2_ = bf16[64,1024]{1,0:T(8,128)(2,1)S(1)} collective-permute-done((bf16[64,1024]{1,0:T(8,128)(2,1)S(1)}, bf16[64,1024]{1,0:T(8,128)(2,1)S(1)}, u32[]{:S(2)}, u32[]{:S(2)}) %collective-permute-start.8) | collective-permute-done | bytes 131104 | tf_op jit(solution)/shard_map/ppermute | solution.py:242
  25.7 0.0 collective-permute-done.7.refs_1_
  25.7 0.3 pack_1.1
  26.0 0.1 collective-permute-start.10
  26.1 0.0 collective-permute-done.6.other_ref.other_tag
  26.1 0.0 slice-done
  26.1 0.0 slice-done.1
  26.1 1.2 %up_first.1.acc_ref = f32[256,2048]{1,0:T(8,128)S(1)} custom-call(bf16[128,1152]{1,0:T(8,128)(2,1)S(1)} %get-tuple-element.33.own_ref.own_tag, bf16[128,1152]{1,0:T(8,128)(2,1)S(1)} %collective-permute-done.6.other_ref.other_tag, bf16[2,2048,1024]{2,1,0:T(8,128)(2,1)S(1)} %bitcast.4), custom_call_target="tpu_custom_call" | custom-call | flops 1073741824 | tf_op jit(solution)/shard_map/up_first/pallas_call | solution.py:23
  27.4 0.2 collective-permute-done.10.other_ref
  27.6 1.6 %up_last.1.hidden_ref = bf16[256,2048]{1,0:T(8,128)(2,1)S(1)} custom-call(bf16[128,1152]{1,0:T(8,128)(2,1)S(1)} %get-tuple-element.33.own_ref.own_tag, bf16[128,1152]{1,0:T(8,128)(2,1)S(1)} %collective-permute-done.6.other_ref.other_tag, bf16[128,1024]{1,0:T(8,128)(2,1)S(1)} %get-tuple-element.36.own_ref, ...), custom_call_target="tpu_custom_call" | custom-call | flops 1073741824 | tf_op jit(solution)/shard_map/up_last/pallas_call | solution.py:23
  29.3 0.0 copy-start.1
  29.3 1.2 %down_1.1 = (bf16[128,1024]{1,0:T(8,128)(2,1)S(1)}, bf16[128,1024]{1,0:T(8,128)(2,1)S(1)}) custom-call(bf16[256,2048]{1,0:T(8,128)(2,1)S(1)} %up_last.1.hidden_ref, bf16[2,1024,2048]{2,1,0:T(8,128)(2,1)S(1)} %get-tuple-element.38.down_ref), custom_call_target="tpu_custom_call" | custom-call | flops 1073741824 | tf_op jit(solution)/shard_map/down_1/pallas_call | solution.py:23
  30.5 0.3 collective-permute-start.15
  30.8 1.2 %down_0.1 = (bf16[128,1024]{1,0:T(8,128)(2,1)S(1)}, bf16[128,1024]{1,0:T(8,128)(2,1)S(1)}) custom-call(bf16[256,2048]{1,0:T(8,128)(2,1)S(1)} %up_last.1.hidden_ref, bf16[2,1024,2048]{2,1,0:T(8,128)(2,1)S(1)} %get-tuple-element.38.down_ref), custom_call_target="tpu_custom_call" | custom-call | flops 1073741824 | tf_op jit(solution)/shard_map/down_0/pallas_call | solution.py:23
  32.1 0.3 collective-permute-start.11
  32.4 0.0 collective-permute-done.15.other_ref
  32.4 0.3 unpack_slots.3
  32.7 2.7 %collective-permute-start.16 = (bf16[64,1024]{1,0:T(8,128)(2,1)S(1)}, bf16[64,1024]{1,0:T(8,128)(2,1)S(1)}, u32[]{:S(2)}, u32[]{:S(2)}) collective-permute-start(bf16[64,1024]{1,0:T(8,128)(2,1)S(1)} %get-tuple-element.48), channel_id=1, source_target_pairs={{0,17},{1,16},{2,19},{3,18},{4,21},{5,20},{6,23},{7,22},{8,14},{9,... | collective-permute-start | bytes 393224 | tf_op jit(solution)/shard_map/ppermute | solution.py:242
  35.4 0.0 collective-permute-start.17
  35.4 1.2 %collective-permute-start.18 = (bf16[64,1024]{1,0:T(8,128)(2,1)S(1)}, bf16[64,1024]{1,0:T(8,128)(2,1)S(1)}, u32[]{:S(2)}, u32[]{:S(2)}) collective-permute-start(bf16[64,1024]{1,0:T(8,128)(2,1)S(1)} %get-tuple-element.50), channel_id=1, source_target_pairs={{0,1},{1,0},{2,3},{3,2},{4,5},{5,4},{6,7},{7,6},{8,10},{9,11},{10,... | collective-permute-start | bytes 393224 | tf_op jit(solution)/shard_map/ppermute | solution.py:242
  36.6 0.0 collective-permute-done.11.other_ref
  36.6 0.3 unpack_slots.2
  36.9 2.4 %collective-permute-start.12 = (bf16[64,1024]{1,0:T(8,128)(2,1)S(1)}, bf16[64,1024]{1,0:T(8,128)(2,1)S(1)}, u32[]{:S(2)}, u32[]{:S(2)}) collective-permute-start(bf16[64,1024]{1,0:T(8,128)(2,1)S(1)} %get-tuple-element.42), channel_id=1, source_target_pairs={{0,17},{1,16},{2,19},{3,18},{4,21},{5,20},{6,23},{7,22},{8,14},{9,... | collective-permute-start | bytes 393224 | tf_op jit(solution)/shard_map/ppermute | solution.py:242
  39.2 0.0 collective-permute-start.13
  39.2 0.0 collective-permute-done.16.refs_5_
  39.2 1.2 %collective-permute-start.14 = (bf16[64,1024]{1,0:T(8,128)(2,1)S(1)}, bf16[64,1024]{1,0:T(8,128)(2,1)S(1)}, u32[]{:S(2)}, u32[]{:S(2)}) collective-permute-start(bf16[64,1024]{1,0:T(8,128)(2,1)S(1)} %get-tuple-element.44), channel_id=1, source_target_pairs={{0,1},{1,0},{2,3},{3,2},{4,5},{5,4},{6,7},{7,6},{8,10},{9,11},{10,... | collective-permute-start | bytes 393224 | tf_op jit(solution)/shard_map/ppermute | solution.py:242
  40.4 0.0 collective-permute-done.17.refs_6_
  40.4 0.5 %collective-permute-done.18.refs_7_ = bf16[64,1024]{1,0:T(8,128)(2,1)S(1)} collective-permute-done((bf16[64,1024]{1,0:T(8,128)(2,1)S(1)}, bf16[64,1024]{1,0:T(8,128)(2,1)S(1)}, u32[]{:S(2)}, u32[]{:S(2)}) %collective-permute-start.18) | collective-permute-done | bytes 131104 | tf_op jit(solution)/shard_map/ppermute | solution.py:242
  40.9 2.3 %collective-permute-done.12.refs_1_ = bf16[64,1024]{1,0:T(8,128)(2,1)S(1)} collective-permute-done((bf16[64,1024]{1,0:T(8,128)(2,1)S(1)}, bf16[64,1024]{1,0:T(8,128)(2,1)S(1)}, u32[]{:S(2)}, u32[]{:S(2)}) %collective-permute-start.12) | collective-permute-done | bytes 131104 | tf_op jit(solution)/shard_map/ppermute | solution.py:242
  43.3 1.4 %collective-permute-done.13.refs_2_ = bf16[64,1024]{1,0:T(8,128)(2,1)S(1)} collective-permute-done((bf16[64,1024]{1,0:T(8,128)(2,1)S(1)}, bf16[64,1024]{1,0:T(8,128)(2,1)S(1)}, u32[]{:S(2)}, u32[]{:S(2)}) %collective-permute-start.13) | collective-permute-done | bytes 131104 | tf_op jit(solution)/shard_map/ppermute | solution.py:242
  44.6 0.2 collective-permute-done.14.refs_3_
  44.8 0.1 add_plane.1
  44.9 0.1 collective-permute-start.19
  45.0 1.0 %collective-permute-start.20 = (bf16[16,2048]{1,0:T(8,128)(2,1)S(1)}, bf16[16,2048]{1,0:T(8,128)(2,1)S(1)}, u32[]{:S(2)}, u32[]{:S(2)}) collective-permute-start(bf16[16,2048]{1,0:T(8,128)(2,1)S(1)} %get-tuple-element.53), channel_id=1, source_target_pairs={{0,4},{1,5},{2,6},{3,7},{4,0},{5,1},{6,2},{7,3},{8,24},{9,25},{10,... | collective-permute-start | bytes 196616 | tf_op jit(solution)/shard_map/ppermute | solution.py:242
  46.0 3.4 %collective-permute-start.21 = (bf16[16,2048]{1,0:T(8,128)(2,1)S(1)}, bf16[16,2048]{1,0:T(8,128)(2,1)S(1)}, u32[]{:S(2)}, u32[]{:S(2)}) collective-permute-start(bf16[16,2048]{1,0:T(8,128)(2,1)S(1)} %get-tuple-element.54), channel_id=1, source_target_pairs={{0,2},{1,3},{2,0},{3,1},{4,6},{5,7},{6,4},{7,5},{8,9},{9,8},{10,11... | collective-permute-start | bytes 196616 | tf_op jit(solution)/shard_map/ppermute | solution.py:242
  49.4 1.7 %collective-permute-done.19.refs_1_ = bf16[16,2048]{1,0:T(8,128)(2,1)S(1)} collective-permute-done((bf16[16,2048]{1,0:T(8,128)(2,1)S(1)}, bf16[16,2048]{1,0:T(8,128)(2,1)S(1)}, u32[]{:S(2)}, u32[]{:S(2)}) %collective-permute-start.19) | collective-permute-done | bytes 65568 | tf_op jit(solution)/shard_map/ppermute | solution.py:242
  51.1 0.0 collective-permute-done.20.refs_2_
  51.1 0.7 %collective-permute-done.21.refs_3_ = bf16[16,2048]{1,0:T(8,128)(2,1)S(1)} collective-permute-done((bf16[16,2048]{1,0:T(8,128)(2,1)S(1)}, bf16[16,2048]{1,0:T(8,128)(2,1)S(1)}, u32[]{:S(2)}, u32[]{:S(2)}) %collective-permute-start.21) | collective-permute-done | bytes 65568 | tf_op jit(solution)/shard_map/ppermute | solution.py:242
  51.8 0.0 copy-done.1
  51.8 0.7 %finish.1 = bf16[16,2048]{1,0:T(8,128)(2,1)} custom-call(f32[1,16]{1,0:T(1,128)S(1)} %bitcast.5, bf16[16,2048]{1,0:T(8,128)(2,1)S(1)} %get-tuple-element.51.refs_0_, bf16[16,2048]{1,0:T(8,128)(2,1)S(1)} %collective-permute-done.19.refs_1_, bf16[16,2048]{1,0:T(8,128)(2,1)S(1)} %collective-permute-done.20.refs_2_, ...), custom_call_target="tpu_custom_call" | custom-call | tf_op jit(solution)/shard_map/finish/pallas_call | solution.py:23
  (3 shorter events, 0.0 us)
Async XLA Ops:
  0.7 0.8 %copy-start = (bf16[16,2048]{1,0:T(8,128)(2,1)S(1)}, bf16[16,2048]{1,0:T(8,128)(2,1)}, u32[]{:S(2)}) copy-start(bf16[16,2048]{1,0:T(8,128)(2,1)} %rows_ref.1) | copy-start | bytes 196612
  1.7 7.5 %collective-permute-start.2 = (bf16[16,2176]{1,0:T(8,128)(2,1)S(1)}, bf16[16,2176]{1,0:T(8,128)(2,1)S(1)}, u32[]{:S(2)}, u32[]{:S(2)}) collective-permute-start(bf16[16,2176]{1,0:T(8,128)(2,1)S(1)} %tag_rows.1.refs_0_), channel_id=1, source_target_pairs={{0,6},{1,7},{2,4},{3,5},{4,2},{5,3},{6,0},{7,1},{8,25},{9,24},{10,... | collective-permute-start | bytes 208904 | tf_op jit(solution)/shard_map/ppermute | solution.py:242
  6.8 5.2 %collective-permute-start.1 = (bf16[16,2176]{1,0:T(8,128)(2,1)S(1)}, bf16[16,2176]{1,0:T(8,128)(2,1)S(1)}, u32[]{:S(2)}, u32[]{:S(2)}) collective-permute-start(bf16[16,2176]{1,0:T(8,128)(2,1)S(1)} %tag_rows.1.refs_0_), channel_id=1, source_target_pairs={{0,4},{1,5},{2,6},{3,7},{4,0},{5,1},{6,2},{7,3},{8,24},{9,25},{10,... | collective-permute-start | bytes 208904 | tf_op jit(solution)/shard_map/ppermute | solution.py:242
  6.8 5.2 %collective-permute-start = (bf16[16,2176]{1,0:T(8,128)(2,1)S(1)}, bf16[16,2176]{1,0:T(8,128)(2,1)S(1)}, u32[]{:S(2)}, u32[]{:S(2)}) collective-permute-start(bf16[16,2176]{1,0:T(8,128)(2,1)S(1)} %tag_rows.1.refs_0_), channel_id=1, source_target_pairs={{0,2},{1,3},{2,0},{3,1},{4,6},{5,7},{6,4},{7,5},{8,9},{9,8},{10,11... | collective-permute-start | bytes 208904 | tf_op jit(solution)/shard_map/ppermute | solution.py:242
  12.0 7.8 %collective-permute-start.5 = (bf16[64,1152]{1,0:T(8,128)(2,1)S(1)}, bf16[64,1152]{1,0:T(8,128)(2,1)S(1)}, u32[]{:S(2)}, u32[]{:S(2)}) collective-permute-start(bf16[64,1152]{1,0:T(8,128)(2,1)S(1)} %get-tuple-element.30.refs_0_), channel_id=1, source_target_pairs={{0,17},{1,16},{2,19},{3,18},{4,21},{5,20},{6,23},{7,22},{8,14},{9,... | collective-permute-start | bytes 442376 | tf_op jit(solution)/shard_map/ppermute | solution.py:242
  16.3 7.6 %collective-permute-start.4 = (bf16[64,1152]{1,0:T(8,128)(2,1)S(1)}, bf16[64,1152]{1,0:T(8,128)(2,1)S(1)}, u32[]{:S(2)}, u32[]{:S(2)}) collective-permute-start(bf16[64,1152]{1,0:T(8,128)(2,1)S(1)} %get-tuple-element.30.refs_0_), channel_id=1, source_target_pairs={{0,16},{1,17},{2,18},{3,19},{4,20},{5,21},{6,22},{7,23},{8,12},{9,... | collective-permute-start | bytes 442376 | tf_op jit(solution)/shard_map/ppermute | solution.py:242
  16.3 7.6 %collective-permute-start.3 = (bf16[64,1152]{1,0:T(8,128)(2,1)S(1)}, bf16[64,1152]{1,0:T(8,128)(2,1)S(1)}, u32[]{:S(2)}, u32[]{:S(2)}) collective-permute-start(bf16[64,1152]{1,0:T(8,128)(2,1)S(1)} %get-tuple-element.30.refs_0_), channel_id=1, source_target_pairs={{0,1},{1,0},{2,3},{3,2},{4,5},{5,4},{6,7},{7,6},{8,10},{9,11},{10,... | collective-permute-start | bytes 442376 | tf_op jit(solution)/shard_map/ppermute | solution.py:242
  16.9 9.2 %slice-start = ((s8[8388608]{0:T(1024)(128)(4,1)}), s8[4194304]{0:T(1024)(128)(4,1)S(1)}, s32[]{:S(2)}) async-start(s8[8388608]{0:T(1024)(128)(4,1)} %bitcast.3), calls=%async_computation | async-start | bytes 8388608
  16.9 7.5 %collective-permute-start.9 = (bf16[64,1024]{1,0:T(8,128)(2,1)S(1)}, bf16[64,1024]{1,0:T(8,128)(2,1)S(1)}, u32[]{:S(2)}, u32[]{:S(2)}) collective-permute-start(bf16[64,1024]{1,0:T(8,128)(2,1)S(1)} %get-tuple-element.35.refs_0_), channel_id=1, source_target_pairs={{0,17},{1,16},{2,19},{3,18},{4,21},{5,20},{6,23},{7,22},{8,14},{9,... | collective-permute-start | bytes 393224 | tf_op jit(solution)/shard_map/ppermute | solution.py:242
  19.8 5.9 %collective-permute-start.8 = (bf16[64,1024]{1,0:T(8,128)(2,1)S(1)}, bf16[64,1024]{1,0:T(8,128)(2,1)S(1)}, u32[]{:S(2)}, u32[]{:S(2)}) collective-permute-start(bf16[64,1024]{1,0:T(8,128)(2,1)S(1)} %get-tuple-element.35.refs_0_), channel_id=1, source_target_pairs={{0,16},{1,17},{2,18},{3,19},{4,20},{5,21},{6,22},{7,23},{8,12},{9,... | collective-permute-start | bytes 393224 | tf_op jit(solution)/shard_map/ppermute | solution.py:242
  19.8 5.9 %collective-permute-start.7 = (bf16[64,1024]{1,0:T(8,128)(2,1)S(1)}, bf16[64,1024]{1,0:T(8,128)(2,1)S(1)}, u32[]{:S(2)}, u32[]{:S(2)}) collective-permute-start(bf16[64,1024]{1,0:T(8,128)(2,1)S(1)} %get-tuple-element.35.refs_0_), channel_id=1, source_target_pairs={{0,1},{1,0},{2,3},{3,2},{4,5},{5,4},{6,7},{7,6},{8,10},{9,11},{10,... | collective-permute-start | bytes 393224 | tf_op jit(solution)/shard_map/ppermute | solution.py:242
  23.9 2.2 %slice-start.1 = ((s8[8388608]{0:T(1024)(128)(4,1)}), s8[4194304]{0:T(1024)(128)(4,1)S(1)}, s32[]{:S(2)}) async-start(s8[8388608]{0:T(1024)(128)(4,1)} %bitcast.3), calls=%async_computation.1 | async-start | bytes 8388608
  24.4 1.7 %collective-permute-start.6 = (bf16[128,1152]{1,0:T(8,128)(2,1)S(1)}, bf16[128,1152]{1,0:T(8,128)(2,1)S(1)}, u32[]{:S(2)}, u32[]{:S(2)}) collective-permute-start(bf16[128,1152]{1,0:T(8,128)(2,1)S(1)} %get-tuple-element.34), channel_id=1, source_target_pairs={{0,8},{8,0},{16,24},{24,16},{1,9},{9,1},{17,25},{25,17},{2,10},{10... | collective-permute-start | bytes 884744 | tf_op jit(solution)/shard_map/ppermute | solution.py:245
  26.0 1.6 %collective-permute-start.10 = (bf16[128,1024]{1,0:T(8,128)(2,1)S(1)}, bf16[128,1024]{1,0:T(8,128)(2,1)S(1)}, u32[]{:S(2)}, u32[]{:S(2)}) collective-permute-start(bf16[128,1024]{1,0:T(8,128)(2,1)S(1)} %get-tuple-element.37), channel_id=1, source_target_pairs={{0,8},{8,0},{16,24},{24,16},{1,9},{9,1},{17,25},{25,17},{2,10},{10... | collective-permute-start | bytes 786440 | tf_op jit(solution)/shard_map/ppermute | solution.py:245
  29.3 22.5 %copy-start.1 = (f32[16]{0:T(128)S(1)}, f32[16]{0:T(128)}, u32[]{:S(2)}) copy-start(f32[16]{0:T(128)} %param.9) | copy-start | bytes 196
  30.5 1.9 %collective-permute-start.15 = (bf16[128,1024]{1,0:T(8,128)(2,1)S(1)}, bf16[128,1024]{1,0:T(8,128)(2,1)S(1)}, u32[]{:S(2)}, u32[]{:S(2)}) collective-permute-start(bf16[128,1024]{1,0:T(8,128)(2,1)S(1)} %get-tuple-element.46), channel_id=1, source_target_pairs={{0,8},{8,0},{16,24},{24,16},{1,9},{9,1},{17,25},{25,17},{2,10},{10... | collective-permute-start | bytes 786440 | tf_op jit(solution)/shard_map/ppermute | solution.py:245
  32.1 4.5 %collective-permute-start.11 = (bf16[128,1024]{1,0:T(8,128)(2,1)S(1)}, bf16[128,1024]{1,0:T(8,128)(2,1)S(1)}, u32[]{:S(2)}, u32[]{:S(2)}) collective-permute-start(bf16[128,1024]{1,0:T(8,128)(2,1)S(1)} %get-tuple-element.40), channel_id=1, source_target_pairs={{0,8},{8,0},{16,24},{24,16},{1,9},{9,1},{17,25},{25,17},{2,10},{10... | collective-permute-start | bytes 786440 | tf_op jit(solution)/shard_map/ppermute | solution.py:245
  32.7 6.5 %collective-permute-start.16 = (bf16[64,1024]{1,0:T(8,128)(2,1)S(1)}, bf16[64,1024]{1,0:T(8,128)(2,1)S(1)}, u32[]{:S(2)}, u32[]{:S(2)}) collective-permute-start(bf16[64,1024]{1,0:T(8,128)(2,1)S(1)} %get-tuple-element.48), channel_id=1, source_target_pairs={{0,17},{1,16},{2,19},{3,18},{4,21},{5,20},{6,23},{7,22},{8,14},{9,... | collective-permute-start | bytes 393224 | tf_op jit(solution)/shard_map/ppermute | solution.py:242
  35.4 5.0 %collective-permute-start.17 = (bf16[64,1024]{1,0:T(8,128)(2,1)S(1)}, bf16[64,1024]{1,0:T(8,128)(2,1)S(1)}, u32[]{:S(2)}, u32[]{:S(2)}) collective-permute-start(bf16[64,1024]{1,0:T(8,128)(2,1)S(1)} %get-tuple-element.49), channel_id=1, source_target_pairs={{0,16},{1,17},{2,18},{3,19},{4,20},{5,21},{6,22},{7,23},{8,12},{9,... | collective-permute-start | bytes 393224 | tf_op jit(solution)/shard_map/ppermute | solution.py:242
  35.4 5.6 %collective-permute-start.18 = (bf16[64,1024]{1,0:T(8,128)(2,1)S(1)}, bf16[64,1024]{1,0:T(8,128)(2,1)S(1)}, u32[]{:S(2)}, u32[]{:S(2)}) collective-permute-start(bf16[64,1024]{1,0:T(8,128)(2,1)S(1)} %get-tuple-element.50), channel_id=1, source_target_pairs={{0,1},{1,0},{2,3},{3,2},{4,5},{5,4},{6,7},{7,6},{8,10},{9,11},{10,... | collective-permute-start | bytes 393224 | tf_op jit(solution)/shard_map/ppermute | solution.py:242
  36.9 6.4 %collective-permute-start.12 = (bf16[64,1024]{1,0:T(8,128)(2,1)S(1)}, bf16[64,1024]{1,0:T(8,128)(2,1)S(1)}, u32[]{:S(2)}, u32[]{:S(2)}) collective-permute-start(bf16[64,1024]{1,0:T(8,128)(2,1)S(1)} %get-tuple-element.42), channel_id=1, source_target_pairs={{0,17},{1,16},{2,19},{3,18},{4,21},{5,20},{6,23},{7,22},{8,14},{9,... | collective-permute-start | bytes 393224 | tf_op jit(solution)/shard_map/ppermute | solution.py:242
  39.2 5.4 %collective-permute-start.13 = (bf16[64,1024]{1,0:T(8,128)(2,1)S(1)}, bf16[64,1024]{1,0:T(8,128)(2,1)S(1)}, u32[]{:S(2)}, u32[]{:S(2)}) collective-permute-start(bf16[64,1024]{1,0:T(8,128)(2,1)S(1)} %get-tuple-element.43), channel_id=1, source_target_pairs={{0,16},{1,17},{2,18},{3,19},{4,20},{5,21},{6,22},{7,23},{8,12},{9,... | collective-permute-start | bytes 393224 | tf_op jit(solution)/shard_map/ppermute | solution.py:242
  39.2 5.6 %collective-permute-start.14 = (bf16[64,1024]{1,0:T(8,128)(2,1)S(1)}, bf16[64,1024]{1,0:T(8,128)(2,1)S(1)}, u32[]{:S(2)}, u32[]{:S(2)}) collective-permute-start(bf16[64,1024]{1,0:T(8,128)(2,1)S(1)} %get-tuple-element.44), channel_id=1, source_target_pairs={{0,1},{1,0},{2,3},{3,2},{4,5},{5,4},{6,7},{7,6},{8,10},{9,11},{10,... | collective-permute-start | bytes 393224 | tf_op jit(solution)/shard_map/ppermute | solution.py:242
  44.9 6.1 %collective-permute-start.19 = (bf16[16,2048]{1,0:T(8,128)(2,1)S(1)}, bf16[16,2048]{1,0:T(8,128)(2,1)S(1)}, u32[]{:S(2)}, u32[]{:S(2)}) collective-permute-start(bf16[16,2048]{1,0:T(8,128)(2,1)S(1)} %get-tuple-element.52), channel_id=1, source_target_pairs={{0,6},{1,7},{2,4},{3,5},{4,2},{5,3},{6,0},{7,1},{8,25},{9,24},{10,... | collective-permute-start | bytes 196616 | tf_op jit(solution)/shard_map/ppermute | solution.py:242
  45.0 6.1 %collective-permute-start.20 = (bf16[16,2048]{1,0:T(8,128)(2,1)S(1)}, bf16[16,2048]{1,0:T(8,128)(2,1)S(1)}, u32[]{:S(2)}, u32[]{:S(2)}) collective-permute-start(bf16[16,2048]{1,0:T(8,128)(2,1)S(1)} %get-tuple-element.53), channel_id=1, source_target_pairs={{0,4},{1,5},{2,6},{3,7},{4,0},{5,1},{6,2},{7,3},{8,24},{9,25},{10,... | collective-permute-start | bytes 196616 | tf_op jit(solution)/shard_map/ppermute | solution.py:242
  46.0 5.7 %collective-permute-start.21 = (bf16[16,2048]{1,0:T(8,128)(2,1)S(1)}, bf16[16,2048]{1,0:T(8,128)(2,1)S(1)}, u32[]{:S(2)}, u32[]{:S(2)}) collective-permute-start(bf16[16,2048]{1,0:T(8,128)(2,1)S(1)} %get-tuple-element.54), channel_id=1, source_target_pairs={{0,2},{1,3},{2,0},{3,1},{4,6},{5,7},{6,4},{7,5},{8,9},{9,8},{10,11... | collective-permute-start | bytes 196616 | tf_op jit(solution)/shard_map/ppermute | solution.py:242
where the time goes:
time: 52.7 us; the launch traced here: 52.5 us
  starting transfers between devices  26.8 us (51%)
  waiting for transfers between devices  12.8 us (24%)
  Pallas kernels  11.2 us (21%)
  local copies, waits for them, and re-layouts  0.86 us (2%)
  other arithmetic  0.68 us (1%)
    ppermute x18, starting transfers between devices, exchange(): return lax.ppermute(value, ('group', 'inner'), pairs)  26 us
    ppermute x18, waiting for transfers between devices, exchange(): return lax.ppermute(value, ('group', 'inner'), pairs)  12.6 us
    pallas_call x13, Pallas kernels, call(): pl.pallas_call(kernel, out_shape=shapes, in_specs=specs or [VMEM_SPEC] *...  11.2 us
  transfers between devices with their start and end apart: 22, of which 10 were waited for; matrix products, arithmetic and copies ran while one was open for 0% of the time, Pallas kernels for 14%

commit v1 on v0

--- a/solution.py
+++ b/solution.py
@@ -68,43 +68,41 @@
         out_refs[0][here, out_refs[0].shape[1] - LANES :] = refs[which][:, full - LANES :]
 
 
-def pack_kernel(capacity, owners, blocks, width, first, *refs):
+def pack_kernel(capacity, blocks, first, *refs):
+    row_refs = refs[:blocks]
     if first:
-        own_ref, other_ref, onehot_ref = refs[blocks + 1 :]
+        own_ref, other_ref, onehot_ref, held = refs[blocks + 1 :]
     else:
-        onehot_ref, own_ref, other_ref = refs[blocks:]
-    block = owners * capacity
-    rows = refs[0].shape[0]
-    count = rows // owners
+        onehot_ref, own_ref, other_ref, held = refs[blocks:]
+    rows, full = row_refs[0].shape
+    half = own_ref.shape[0]
+    for which, ref in enumerate(row_refs):
+        held[which * rows : (which + 1) * rows, :] = ref[...]
     if first:
         me = lax.axis_index("group")
-        col = lax.broadcasted_iota(jnp.int32, (rows, 2 * block), 1)
-        owner_col = (col % block) // capacity
-        owner_row = lax.broadcasted_iota(jnp.int32, (rows, 2 * block), 0) // count
-        wanted = (me ^ (col // block)) * capacity + col % capacity
-    for which in range(blocks):
-        ref = refs[which]
-        here = slice(which * block, (which + 1) * block)
-        if first:
-            tags = ref[:, width:]
-            slot = tags.astype(F32)[:, 0:1].astype(jnp.int32)
-            onehot = ((slot == wanted) & (owner_col == owner_row)).astype(F32).astype(BF16)
+        lane = lax.broadcasted_iota(jnp.int32, (rows, LANES), 1)
+        place = lax.broadcasted_iota(jnp.int32, (rows, 2 * half), 1)
+        down = lax.broadcasted_iota(jnp.int32, (rows, rows), 0)
+        across = lax.broadcasted_iota(jnp.int32, (rows, rows), 1)
+        earlier = (across < down).astype(F32).astype(BF16)
+        taken = jnp.zeros((1, LANES), F32)
+        for which, ref in enumerate(row_refs):
+            tags = ref[:, full - LANES :].astype(F32)
+            group = tags[:, 0:1].astype(jnp.int32) // capacity
+            expert = tags[:, 1:2].astype(jnp.int32) - 1
+            side = jnp.where(group == me, 0, jnp.where(group == (me ^ 1), 1, LANES))
+            named = jnp.where(lane == 2 * side + expert, 1.0, 0.0)
+            ahead = jnp.dot(earlier, named.astype(BF16), preferred_element_type=F32) + taken
+            rank = jnp.sum(named * ahead, axis=1, keepdims=True).astype(jnp.int32)
+            spot = jnp.where(expert == 0, rank, half - 1 - rank) + side * half
+            onehot = (place == spot).astype(F32).astype(BF16)
             onehot_ref[which * rows : (which + 1) * rows, :] = onehot
-        else:
-            onehot = onehot_ref[which * rows : (which + 1) * rows, :]
-
-        def packed(value):
-            return lax.dot_general(
-                onehot, value, (((0,), (0,)), ((), ())), preferred_element_type=F32
-            ).astype(BF16)
-
-        value = packed(ref[:, :width])
-        own_ref[here, :width] = value[:block]
-        other_ref[here, :width] = value[block:]
-        if first:
-            value = packed(tags)
-            own_ref[here, width:] = value[:block]
-            other_ref[here, width:] = value[block:]
+            taken += jnp.sum(named, axis=0, keepdims=True)
+    packed = lax.dot_general(
+        onehot_ref[...], held[...], (((0,), (0,)), ((), ())), preferred_element_type=F32
+    ).astype(BF16)
+    own_ref[...] = packed[:half]
+    other_ref[...] = packed[half:]
 
 
 def load_kernel(after_ref, weight_ref, held_ref, token_ref, sem):
@@ -119,68 +117,95 @@
         copy.wait()
 
 
-def up_product(own_ref, other_ref, up_ref, expert, start, width, cols):
-    rows = jnp.concatenate([own_ref[:, :width], other_ref[:, :width]], axis=0)
-    return jnp.dot(rows, up_ref[expert, start : start + width, cols], preferred_element_type=F32)
+def chosen(own_tag, other_tag):
+    full, half = own_tag.shape[1], own_tag.shape[0]
+    row = lax.broadcasted_iota(jnp.int32, (half, 1), 0)
+    parts, crossed = [], 0.0
+    for ref in (own_tag, other_tag):
+        part = ref[:, full - LANES :].astype(F32)[:, 1:2]
+        wrong = ((part == 1.0) & (row >= half // 2)) | ((part == 2.0) & (row < half // 2))
+        crossed = jnp.maximum(crossed, jnp.max(jnp.where(wrong, 1.0, 0.0)))
+        parts.append(part)
+    return jnp.concatenate(parts, axis=0), crossed > 0.0
+
+
+def by_expert(own_tag, other_tag, pieces, product, store):
+    half = own_tag.shape[0]
+    fit = half // 2
+    tags, crossed = chosen(own_tag, other_tag)
+
+    @pl.when(jnp.logical_not(crossed))
+    def _():
+        for expert in range(2):
+            here = slice(expert * fit, (expert + 1) * fit)
+            for piece in range(pieces):
+                value = product(expert, piece, here)
+                store(piece, here, value[:fit], value[fit:])
+
+    @pl.when(crossed)
+    def _():
+        here = slice(0, half)
+        for piece in range(pieces):
+            value = jnp.where(tags == 2.0, product(1, piece, here), product(0, piece, here))
+            store(piece, here, value[:half], value[half:])
 
 
 def up_first_kernel(step, width, own_ref, other_ref, up_ref, acc_ref):
-    experts, _, units = up_ref.shape
-    for expert in range(experts):
-        for at in range(0, units, step):
-            acc_ref[:, expert * units + at : expert * units + at + step] = up_product(
-                own_ref, other_ref, up_ref, expert, 0, width, slice(at, at + step)
-            )
+    half = own_ref.shape[0]
+
+    def product(expert, piece, here):
+        rows = jnp.concatenate([own_ref[here, :width], other_ref[here, :width]], axis=0)
+        cols = slice(piece * step, (piece + 1) * step)
+        return jnp.dot(rows, up_ref[expert, :width, cols], preferred_element_type=F32)
+
+    def store(piece, here, own, other):
+        cols = slice(piece * step, (piece + 1) * step)
+        acc_ref[here, cols] = own
+        acc_ref[half + here.start : half + here.stop, cols] = other
+
+    by_expert(own_ref, other_ref, up_ref.shape[2] // step, product, store)
 
 
 def up_last_kernel(step, start, width, own_tag, other_tag, own_ref, other_ref, up_ref, acc_ref, hidden_ref):
-    experts, _, units = up_ref.shape
-    full = own_tag.shape[1]
-    chosen = jnp.concatenate(
-        [own_tag[:, full - LANES :].astype(F32)[:, 1:2], other_tag[:, full - LANES :].astype(F32)[:, 1:2]],
-        axis=0,
-    )
-    for expert in range(experts):
-        mine = chosen == float(expert + 1)
-        for at in range(0, units, step):
-            cols = slice(expert * units + at, expert * units + at + step)
-            value = acc_ref[:, cols] + up_product(
-                own_ref, other_ref, up_ref, expert, start, width, slice(at, at + step)
-            )
-            value = jnp.where(mine, value / (1.0 + jnp.exp(-value)), 0.0)
-            hidden_ref[:, cols] = value.astype(BF16)
-
-
-def down_kernel(step, start, width, hidden_ref, down_ref, own_ref, other_ref):
-    experts, units, _ = down_ref.shape
     half = own_ref.shape[0]
-    for at in range(0, width, step):
-        total = None
-        for expert in range(experts):
-            term = jnp.dot(
-                hidden_ref[:, expert * units : (expert + 1) * units],
-                down_ref[expert, :, start + at : start + at + step],
-                preferred_element_type=F32,
-            )
-            total = term if total is None else total + term
-        total = total.astype(BF16)
-        own_ref[:, at : at + step] = total[:half]
-        other_ref[:, at : at + step] = total[half:]
-
-
-def dense_block(which, block, rows, onehot_ref, own_ref, other_ref):
-    here = slice(which * block, (which + 1) * block)
-    slots = jnp.concatenate([own_ref[here, :], other_ref[here, :]], axis=0)
-    onehot = onehot_ref[which * rows : (which + 1) * rows, :]
-    return jnp.dot(onehot, slots, preferred_element_type=F32).astype(BF16)
+
+    def product(expert, piece, here):
+        rows = jnp.concatenate([own_ref[here, :width], other_ref[here, :width]], axis=0)
+        cols = slice(piece * step, (piece + 1) * step)
+        return jnp.dot(rows, up_ref[expert, start : start + width, cols], preferred_element_type=F32)
+
+    def store(piece, here, own, other):
+        cols = slice(piece * step, (piece + 1) * step)
+        for offset, value in ((0, own), (half, other)):
+            rows = slice(offset + here.start, offset + here.stop)
+            value = acc_ref[rows, cols] + value
+            hidden_ref[rows, cols] = (value / (1.0 + jnp.exp(-value))).astype(BF16)
+
+    by_expert(own_tag, other_tag, up_ref.shape[2] // step, product, store)
+
+
+def down_kernel(step, start, width, own_tag, other_tag, hidden_ref, down_ref, own_ref, other_ref):
+    half = own_ref.shape[0]
+
+    def product(expert, piece, here):
+        rows = jnp.concatenate(
+            [hidden_ref[here, :], hidden_ref[half + here.start : half + here.stop, :]], axis=0
+        )
+        cols = slice(start + piece * step, start + (piece + 1) * step)
+        return jnp.dot(rows, down_ref[expert, :, cols], preferred_element_type=F32)
+
+    def store(piece, here, own, other):
+        cols = slice(piece * step, (piece + 1) * step)
+        own_ref[here, cols] = own.astype(BF16)
+        other_ref[here, cols] = other.astype(BF16)
+
+    by_expert(own_tag, other_tag, width // step, product, store)
 
 
 def unpack_kernel(onehot_ref, own_ref, other_ref, *out_refs):
-    block = onehot_ref.shape[1] // 2
     rows = out_refs[0].shape[0]
+    slots = jnp.concatenate([own_ref[...], other_ref[...]], axis=0)
     for which, out_ref in enumerate(out_refs):
-        here = slice(which * block, (which + 1) * block)
-        slots = jnp.concatenate([own_ref[here, :], other_ref[here, :]], axis=0)
         onehot = onehot_ref[which * rows : (which + 1) * rows, :]
         out_ref[...] = jnp.dot(onehot, slots, preferred_element_type=F32).astype(BF16)
 
@@ -263,6 +288,7 @@
         flops=STACK_FLOPS,
     )
 
+    room = 4 + 8 * blocks * rows * half * 2 * 2 // MIB
     onehot = None
     slots = []
     for chunk, width in enumerate(widths):
@@ -281,12 +307,14 @@
             )
         outs = [((half, width + LANES * first), BF16)] * 2
         if first:
-            outs.append(((blocks * rows, 2 * block), BF16))
+            outs.append(((blocks * rows, 2 * half), BF16))
         packed = call(
-            functools.partial(pack_kernel, capacity, far, blocks, width, first),
+            functools.partial(pack_kernel, capacity, blocks, first),
             f"pack_{chunk}",
             outs,
             [*arrived, down_token] if first else [*arrived, onehot],
+            scratch=[pltpu.VMEM((blocks * rows, parts[chunk].shape[1]), BF16)],
+            limit=room,
             flops=PACK_FLOPS,
         )
         if first:
@@ -297,7 +325,7 @@
     acc = call(
         functools.partial(up_first_kernel, step, widths[0]),
         "up_first",
-        [((2 * half, experts * units), F32)],
+        [((2 * half, units), F32)],
         [*slots[0], w_up],
         limit=8,
         flops=work * widths[0],
@@ -305,7 +333,7 @@
     (hidden,) = call(
         functools.partial(up_last_kernel, step, starts[1], widths[1]),
         "up_last",
-        [((2 * half, experts * units), BF16)],
+        [((2 * half, units), BF16)],
         [*slots[0], *slots[1], w_up, acc],
         limit=8,
         flops=work * widths[1],
@@ -318,7 +346,7 @@
             functools.partial(down_kernel, min(256, width), starts[chunk], width),
             f"down_{chunk}",
             [((half, width), BF16)] * 2,
-            [hidden, down_held],
+            [*slots[0], hidden, down_held],
             limit=8,
             flops=work * width,
         )
@@ -327,6 +355,7 @@
             "unpack_slots",
             [((rows, width), BF16)] * blocks,
             [onehot, own, along_group(other, 1)],
+            limit=room,
         )
         terms[chunk] = [dense[0]] + [exchange(dense[s], True, s) for s in range(blocks - 1, 0, -1)]
     sums = call(

time: 52.7 us -> 52.6 us (level); the launches traced: 52.5 us -> 51.6 us
  Pallas kernels: 11.2 us -> 10.3 us
    pallas_call x13, Pallas kernels: 11.2 us -> 10.3 us  [call(): pl.pallas_call(kernel, out_shape=shapes, in_specs=specs or [VMEM_SPEC] *...]
  transfers between devices with their start and end apart: 22 -> 22, of which waited for: 10 -> 12; matrix products, arithmetic and copies ran while one was open for 0% -> 0% of each run, Pallas kernels for 14% -> 14%
where the time goes in v1:
time: 52.6 us; the launch traced here: 51.6 us
  starting transfers between devices  26.7 us (51%)
  waiting for transfers between devices  12.8 us (24%)
  Pallas kernels  10.3 us (20%)
  local copies, waits for them, and re-layouts  0.86 us (2%)
  other arithmetic  0.68 us (1%)
    ppermute x18, starting transfers between devices, exchange(): return lax.ppermute(value, ('group', 'inner'), pairs)  26 us
    ppermute x18, waiting for transfers between devices, exchange(): return lax.ppermute(value, ('group', 'inner'), pairs)  12.1 us
    pallas_call x13, Pallas kernels, call(): pl.pallas_call(kernel, out_shape=shapes, in_specs=specs or [VMEM_SPEC] *...  10.3 us
  transfers between devices with their start and end apart: 22, of which 12 were waited for; matrix products, arithmetic and copies ran while one was open for 0% of the time, Pallas kernels for 14%

profile of v1, /device:TPU:0, one launch (start us, length us, event | category | flops | bytes accessed | tf_op | source)
XLA Modules:
  0.0 51.6 jit_solution(9926292477308739856)
XLA Ops:
  0.0 0.7 %add_bitcast_fusion.expert_ref = s32[1,16]{1,0:T(1,128)S(1)} fusion(s32[16,1]{0,1:T(1,128)} %param.8, s32[16,1]{0,1:T(1,128)} %param.7), kind=kLoop, calls=%fused_computation | loop fusion | flops 32 | bytes 192 | tf_op jit(solution)/shard_map/reshape | solution.py:278
  0.7 0.0 copy-start
  0.7 0.8 %copy-done = bf16[16,2048]{1,0:T(8,128)(2,1)S(1)} copy-done((bf16[16,2048]{1,0:T(8,128)(2,1)S(1)}, bf16[16,2048]{1,0:T(8,128)(2,1)}, u32[]{:S(2)}) %copy-start) | copy-done | bytes 65560
  1.5 0.2 tag_rows.1.refs_0_
  1.7 5.1 %collective-permute-start.2 = (bf16[16,2176]{1,0:T(8,128)(2,1)S(1)}, bf16[16,2176]{1,0:T(8,128)(2,1)S(1)}, u32[]{:S(2)}, u32[]{:S(2)}) collective-permute-start(bf16[16,2176]{1,0:T(8,128)(2,1)S(1)} %tag_rows.1.refs_0_), channel_id=1, source_target_pairs={{0,6},{1,7},{2,4},{3,5},{4,2},{5,3},{6,0},{7,1},{8,25},{9,24},{10,... | collective-permute-start | bytes 208904 | tf_op jit(solution)/shard_map/ppermute | solution.py:267
  6.8 0.0 collective-permute-start.1
  6.8 0.6 %collective-permute-start = (bf16[16,2176]{1,0:T(8,128)(2,1)S(1)}, bf16[16,2176]{1,0:T(8,128)(2,1)S(1)}, u32[]{:S(2)}, u32[]{:S(2)}) collective-permute-start(bf16[16,2176]{1,0:T(8,128)(2,1)S(1)} %tag_rows.1.refs_0_), channel_id=1, source_target_pairs={{0,2},{1,3},{2,0},{3,1},{4,6},{5,7},{6,4},{7,5},{8,9},{9,8},{10,11... | collective-permute-start | bytes 208904 | tf_op jit(solution)/shard_map/ppermute | solution.py:267
  7.4 1.8 %collective-permute-done.2.refs_3_ = bf16[16,2176]{1,0:T(8,128)(2,1)S(1)} collective-permute-done((bf16[16,2176]{1,0:T(8,128)(2,1)S(1)}, bf16[16,2176]{1,0:T(8,128)(2,1)S(1)}, u32[]{:S(2)}, u32[]{:S(2)}) %collective-permute-start.2) | collective-permute-done | bytes 69664 | tf_op jit(solution)/shard_map/ppermute | solution.py:267
  9.2 2.8 %collective-permute-done.1.refs_2_ = bf16[16,2176]{1,0:T(8,128)(2,1)S(1)} collective-permute-done((bf16[16,2176]{1,0:T(8,128)(2,1)S(1)}, bf16[16,2176]{1,0:T(8,128)(2,1)S(1)}, u32[]{:S(2)}, u32[]{:S(2)}) %collective-permute-start.1) | collective-permute-done | bytes 69664 | tf_op jit(solution)/shard_map/ppermute | solution.py:267
  12.0 0.0 collective-permute-done.refs_1_
  12.0 4.3 %collective-permute-start.5 = (bf16[64,1152]{1,0:T(8,128)(2,1)S(1)}, bf16[64,1152]{1,0:T(8,128)(2,1)S(1)}, u32[]{:S(2)}, u32[]{:S(2)}) collective-permute-start(bf16[64,1152]{1,0:T(8,128)(2,1)S(1)} %get-tuple-element.30.refs_0_), channel_id=1, source_target_pairs={{0,17},{1,16},{2,19},{3,18},{4,21},{5,20},{6,23},{7,22},{8,14},{9,... | collective-permute-start | bytes 442376 | tf_op jit(solution)/shard_map/ppermute | solution.py:267
  16.3 0.0 collective-permute-start.4
  16.3 0.6 %collective-permute-start.3 = (bf16[64,1152]{1,0:T(8,128)(2,1)S(1)}, bf16[64,1152]{1,0:T(8,128)(2,1)S(1)}, u32[]{:S(2)}, u32[]{:S(2)}) collective-permute-start(bf16[64,1152]{1,0:T(8,128)(2,1)S(1)} %get-tuple-element.30.refs_0_), channel_id=1, source_target_pairs={{0,1},{1,0},{2,3},{3,2},{4,5},{5,4},{6,7},{7,6},{8,10},{9,11},{10,... | collective-permute-start | bytes 442376 | tf_op jit(solution)/shard_map/ppermute | solution.py:267
  16.9 2.8 %collective-permute-start.9 = (bf16[64,1024]{1,0:T(8,128)(2,1)S(1)}, bf16[64,1024]{1,0:T(8,128)(2,1)S(1)}, u32[]{:S(2)}, u32[]{:S(2)}) collective-permute-start(bf16[64,1024]{1,0:T(8,128)(2,1)S(1)} %get-tuple-element.35.refs_0_), channel_id=1, source_target_pairs={{0,17},{1,16},{2,19},{3,18},{4,21},{5,20},{6,23},{7,22},{8,14},{9,... | collective-permute-start | bytes 393224 | tf_op jit(solution)/shard_map/ppermute | solution.py:267
  19.8 0.0 collective-permute-start.8
  19.8 0.0 collective-permute-done.5.after_ref.refs_3_
  19.8 0.6 %collective-permute-start.7 = (bf16[64,1024]{1,0:T(8,128)(2,1)S(1)}, bf16[64,1024]{1,0:T(8,128)(2,1)S(1)}, u32[]{:S(2)}, u32[]{:S(2)}) collective-permute-start(bf16[64,1024]{1,0:T(8,128)(2,1)S(1)} %get-tuple-element.35.refs_0_), channel_id=1, source_target_pairs={{0,1},{1,0},{2,3},{3,2},{4,5},{5,4},{6,7},{7,6},{8,10},{9,11},{10,... | collective-permute-start | bytes 393224 | tf_op jit(solution)/shard_map/ppermute | solution.py:267
  20.4 3.5 %load_down.1 = (bf16[2,1024,2048]{2,1,0:T(8,128)(2,1)S(1)}, f32[8,128]{1,0:T(8,128)S(1)}) custom-call(bf16[64,1152]{1,0:T(8,128)(2,1)S(1)} %collective-permute-done.5.after_ref.refs_3_, bf16[2,1024,2048]{2,1,0:T(8,128)(2,1)} %weight_ref.1), custom_call_target="tpu_custom_call" | custom-call | bytes 16777216 | tf_op jit(solution)/shard_map/load_down/pallas_call | solution.py:23
  23.9 0.0 collective-permute-done.4.refs_2_
  23.9 0.0 collective-permute-done.3.refs_1_
  23.9 0.0 slice-start.1
  24.0 0.9 %pack_0.1 = (bf16[128,1152]{1,0:T(8,128)(2,1)S(1)}, bf16[128,1152]{1,0:T(8,128)(2,1)S(1)}, bf16[256,256]{1,0:T(8,128)(2,1)S(1)}) custom-call(bf16[64,1152]{1,0:T(8,128)(2,1)S(1)} %get-tuple-element.30.refs_0_, bf16[64,1152]{1,0:T(8,128)(2,1)S(1)} %collective-permute-done.3.refs_1_, bf16[64,1152]{1,0:T(8,128)(2,1)S(1)} %collective-permute-done.4.refs_2_, ...), custom_call_target="tpu_custom_call" | custom-call | flops 1500000000 | tf_op jit(solution)/shard_map/pack_0/pallas_call | solution.py:23
  24.8 0.1 collective-permute-start.6
  24.9 0.0 collective-permute-done.9.refs_3_
  24.9 0.8 %collective-permute-done.8.refs_2_ = bf16[64,1024]{1,0:T(8,128)(2,1)S(1)} collective-permute-done((bf16[64,1024]{1,0:T(8,128)(2,1)S(1)}, bf16[64,1024]{1,0:T(8,128)(2,1)S(1)}, u32[]{:S(2)}, u32[]{:S(2)}) %collective-permute-start.8) | collective-permute-done | bytes 131104 | tf_op jit(solution)/shard_map/ppermute | solution.py:267
  25.7 0.0 collective-permute-done.7.refs_1_
  25.7 0.3 pack_1.1
  26.0 0.1 collective-permute-start.10
  26.1 0.4 collective-permute-done.6.other_ref.other_tag
  26.5 0.0 slice-done
  26.5 0.0 slice-done.1
  26.5 0.9 %up_first.1.acc_ref = f32[256,1024]{1,0:T(8,128)S(1)} custom-call(bf16[128,1152]{1,0:T(8,128)(2,1)S(1)} %get-tuple-element.33.own_ref.own_tag, bf16[128,1152]{1,0:T(8,128)(2,1)S(1)} %collective-permute-done.6.other_ref.other_tag, bf16[2,2048,1024]{2,1,0:T(8,128)(2,1)S(1)} %bitcast.4), custom_call_target="tpu_custom_call" | custom-call | flops 1073741824 | tf_op jit(solution)/shard_map/up_first/pallas_call | solution.py:23
  27.4 0.3 collective-permute-done.10.other_ref
  27.6 1.0 %up_last.1.hidden_ref = bf16[256,1024]{1,0:T(8,128)(2,1)S(1)} custom-call(bf16[128,1152]{1,0:T(8,128)(2,1)S(1)} %get-tuple-element.33.own_ref.own_tag, bf16[128,1152]{1,0:T(8,128)(2,1)S(1)} %collective-permute-done.6.other_ref.other_tag, bf16[128,1024]{1,0:T(8,128)(2,1)S(1)} %get-tuple-element.36.own_ref, ...), custom_call_target="tpu_custom_call" | custom-call | flops 1073741824 | tf_op jit(solution)/shard_map/up_last/pallas_call | solution.py:23
  28.6 0.0 copy-start.1
  28.6 0.9 %down_1.1 = (bf16[128,1024]{1,0:T(8,128)(2,1)S(1)}, bf16[128,1024]{1,0:T(8,128)(2,1)S(1)}) custom-call(bf16[128,1152]{1,0:T(8,128)(2,1)S(1)} %get-tuple-element.33.own_ref.own_tag, bf16[128,1152]{1,0:T(8,128)(2,1)S(1)} %collective-permute-done.6.other_ref.other_tag, bf16[256,1024]{1,0:T(8,128)(2,1)S(1)} %up_last.1.hidden_ref, ...), custom_call_target="tpu_custom_call" | custom-call | flops 1073741824 | tf_op jit(solution)/shard_map/down_1/pallas_call | solution.py:23
  29.6 0.2 collective-permute-start.15
  29.7 0.9 %down_0.1 = (bf16[128,1024]{1,0:T(8,128)(2,1)S(1)}, bf16[128,1024]{1,0:T(8,128)(2,1)S(1)}) custom-call(bf16[128,1152]{1,0:T(8,128)(2,1)S(1)} %get-tuple-element.33.own_ref.own_tag, bf16[128,1152]{1,0:T(8,128)(2,1)S(1)} %collective-permute-done.6.other_ref.other_tag, bf16[256,1024]{1,0:T(8,128)(2,1)S(1)} %up_last.1.hidden_ref, ...), custom_call_target="tpu_custom_call" | custom-call | flops 1073741824 | tf_op jit(solution)/shard_map/down_0/pallas_call | solution.py:23
  30.6 0.4 collective-permute-start.11
  31.1 0.1 collective-permute-done.15.other_ref
  31.2 0.5 unpack_slots.3
  31.6 2.7 %collective-permute-start.16 = (bf16[64,1024]{1,0:T(8,128)(2,1)S(1)}, bf16[64,1024]{1,0:T(8,128)(2,1)S(1)}, u32[]{:S(2)}, u32[]{:S(2)}) collective-permute-start(bf16[64,1024]{1,0:T(8,128)(2,1)S(1)} %get-tuple-element.48), channel_id=1, source_target_pairs={{0,17},{1,16},{2,19},{3,18},{4,21},{5,20},{6,23},{7,22},{8,14},{9,... | collective-permute-start | bytes 393224 | tf_op jit(solution)/shard_map/ppermute | solution.py:267
  34.3 0.0 collective-permute-start.17
  34.3 1.2 %collective-permute-start.18 = (bf16[64,1024]{1,0:T(8,128)(2,1)S(1)}, bf16[64,1024]{1,0:T(8,128)(2,1)S(1)}, u32[]{:S(2)}, u32[]{:S(2)}) collective-permute-start(bf16[64,1024]{1,0:T(8,128)(2,1)S(1)} %get-tuple-element.50), channel_id=1, source_target_pairs={{0,1},{1,0},{2,3},{3,2},{4,5},{5,4},{6,7},{7,6},{8,10},{9,11},{10,... | collective-permute-start | bytes 393224 | tf_op jit(solution)/shard_map/ppermute | solution.py:267
  35.5 0.0 collective-permute-done.11.other_ref
  35.5 0.5 unpack_slots.2
  36.0 2.4 %collective-permute-start.12 = (bf16[64,1024]{1,0:T(8,128)(2,1)S(1)}, bf16[64,1024]{1,0:T(8,128)(2,1)S(1)}, u32[]{:S(2)}, u32[]{:S(2)}) collective-permute-start(bf16[64,1024]{1,0:T(8,128)(2,1)S(1)} %get-tuple-element.42), channel_id=1, source_target_pairs={{0,17},{1,16},{2,19},{3,18},{4,21},{5,20},{6,23},{7,22},{8,14},{9,... | collective-permute-start | bytes 393224 | tf_op jit(solution)/shard_map/ppermute | solution.py:267
  38.3 0.0 collective-permute-start.13
  38.3 0.0 collective-permute-done.16.refs_5_
  38.3 1.2 %collective-permute-start.14 = (bf16[64,1024]{1,0:T(8,128)(2,1)S(1)}, bf16[64,1024]{1,0:T(8,128)(2,1)S(1)}, u32[]{:S(2)}, u32[]{:S(2)}) collective-permute-start(bf16[64,1024]{1,0:T(8,128)(2,1)S(1)} %get-tuple-element.44), channel_id=1, source_target_pairs={{0,1},{1,0},{2,3},{3,2},{4,5},{5,4},{6,7},{7,6},{8,10},{9,11},{10,... | collective-permute-start | bytes 393224 | tf_op jit(solution)/shard_map/ppermute | solution.py:267
  39.5 0.0 collective-permute-done.17.refs_6_
  39.5 0.3 collective-permute-done.18.refs_7_
  39.9 2.3 %collective-permute-done.12.refs_1_ = bf16[64,1024]{1,0:T(8,128)(2,1)S(1)} collective-permute-done((bf16[64,1024]{1,0:T(8,128)(2,1)S(1)}, bf16[64,1024]{1,0:T(8,128)(2,1)S(1)}, u32[]{:S(2)}, u32[]{:S(2)}) %collective-permute-start.12) | collective-permute-done | bytes 131104 | tf_op jit(solution)/shard_map/ppermute | solution.py:267
  42.2 1.4 %collective-permute-done.13.refs_2_ = bf16[64,1024]{1,0:T(8,128)(2,1)S(1)} collective-permute-done((bf16[64,1024]{1,0:T(8,128)(2,1)S(1)}, bf16[64,1024]{1,0:T(8,128)(2,1)S(1)}, u32[]{:S(2)}, u32[]{:S(2)}) %collective-permute-start.13) | collective-permute-done | bytes 131104 | tf_op jit(solution)/shard_map/ppermute | solution.py:267
  43.5 0.4 collective-permute-done.14.refs_3_
  43.9 0.1 add_plane.1
  44.0 0.1 collective-permute-start.19
  44.1 1.0 %collective-permute-start.20 = (bf16[16,2048]{1,0:T(8,128)(2,1)S(1)}, bf16[16,2048]{1,0:T(8,128)(2,1)S(1)}, u32[]{:S(2)}, u32[]{:S(2)}) collective-permute-start(bf16[16,2048]{1,0:T(8,128)(2,1)S(1)} %get-tuple-element.53), channel_id=1, source_target_pairs={{0,4},{1,5},{2,6},{3,7},{4,0},{5,1},{6,2},{7,3},{8,24},{9,25},{10,... | collective-permute-start | bytes 196616 | tf_op jit(solution)/shard_map/ppermute | solution.py:267
  45.1 3.4 %collective-permute-start.21 = (bf16[16,2048]{1,0:T(8,128)(2,1)S(1)}, bf16[16,2048]{1,0:T(8,128)(2,1)S(1)}, u32[]{:S(2)}, u32[]{:S(2)}) collective-permute-start(bf16[16,2048]{1,0:T(8,128)(2,1)S(1)} %get-tuple-element.54), channel_id=1, source_target_pairs={{0,2},{1,3},{2,0},{3,1},{4,6},{5,7},{6,4},{7,5},{8,9},{9,8},{10,11... | collective-permute-start | bytes 196616 | tf_op jit(solution)/shard_map/ppermute | solution.py:267
  48.5 1.7 %collective-permute-done.19.refs_1_ = bf16[16,2048]{1,0:T(8,128)(2,1)S(1)} collective-permute-done((bf16[16,2048]{1,0:T(8,128)(2,1)S(1)}, bf16[16,2048]{1,0:T(8,128)(2,1)S(1)}, u32[]{:S(2)}, u32[]{:S(2)}) %collective-permute-start.19) | collective-permute-done | bytes 65568 | tf_op jit(solution)/shard_map/ppermute | solution.py:267
  50.2 0.0 collective-permute-done.20.refs_2_
  50.2 0.7 %collective-permute-done.21.refs_3_ = bf16[16,2048]{1,0:T(8,128)(2,1)S(1)} collective-permute-done((bf16[16,2048]{1,0:T(8,128)(2,1)S(1)}, bf16[16,2048]{1,0:T(8,128)(2,1)S(1)}, u32[]{:S(2)}, u32[]{:S(2)}) %collective-permute-start.21) | collective-permute-done | bytes 65568 | tf_op jit(solution)/shard_map/ppermute | solution.py:267
  50.9 0.0 copy-done.1
  50.9 0.7 %finish.1 = bf16[16,2048]{1,0:T(8,128)(2,1)} custom-call(f32[1,16]{1,0:T(1,128)S(1)} %bitcast.5, bf16[16,2048]{1,0:T(8,128)(2,1)S(1)} %get-tuple-element.51.refs_0_, bf16[16,2048]{1,0:T(8,128)(2,1)S(1)} %collective-permute-done.19.refs_1_, bf16[16,2048]{1,0:T(8,128)(2,1)S(1)} %collective-permute-done.20.refs_2_, ...), custom_call_target="tpu_custom_call" | custom-call | tf_op jit(solution)/shard_map/finish/pallas_call | solution.py:23
  (3 shorter events, 0.0 us)
Async XLA Ops:
  0.7 0.8 %copy-start = (bf16[16,2048]{1,0:T(8,128)(2,1)S(1)}, bf16[16,2048]{1,0:T(8,128)(2,1)}, u32[]{:S(2)}) copy-start(bf16[16,2048]{1,0:T(8,128)(2,1)} %rows_ref.1) | copy-start | bytes 196612
  1.7 7.5 %collective-permute-start.2 = (bf16[16,2176]{1,0:T(8,128)(2,1)S(1)}, bf16[16,2176]{1,0:T(8,128)(2,1)S(1)}, u32[]{:S(2)}, u32[]{:S(2)}) collective-permute-start(bf16[16,2176]{1,0:T(8,128)(2,1)S(1)} %tag_rows.1.refs_0_), channel_id=1, source_target_pairs={{0,6},{1,7},{2,4},{3,5},{4,2},{5,3},{6,0},{7,1},{8,25},{9,24},{10,... | collective-permute-start | bytes 208904 | tf_op jit(solution)/shard_map/ppermute | solution.py:267
  6.8 5.2 %collective-permute-start.1 = (bf16[16,2176]{1,0:T(8,128)(2,1)S(1)}, bf16[16,2176]{1,0:T(8,128)(2,1)S(1)}, u32[]{:S(2)}, u32[]{:S(2)}) collective-permute-start(bf16[16,2176]{1,0:T(8,128)(2,1)S(1)} %tag_rows.1.refs_0_), channel_id=1, source_target_pairs={{0,4},{1,5},{2,6},{3,7},{4,0},{5,1},{6,2},{7,3},{8,24},{9,25},{10,... | collective-permute-start | bytes 208904 | tf_op jit(solution)/shard_map/ppermute | solution.py:267
  6.8 5.2 %collective-permute-start = (bf16[16,2176]{1,0:T(8,128)(2,1)S(1)}, bf16[16,2176]{1,0:T(8,128)(2,1)S(1)}, u32[]{:S(2)}, u32[]{:S(2)}) collective-permute-start(bf16[16,2176]{1,0:T(8,128)(2,1)S(1)} %tag_rows.1.refs_0_), channel_id=1, source_target_pairs={{0,2},{1,3},{2,0},{3,1},{4,6},{5,7},{6,4},{7,5},{8,9},{9,8},{10,11... | collective-permute-start | bytes 208904 | tf_op jit(solution)/shard_map/ppermute | solution.py:267
  12.0 7.8 %collective-permute-start.5 = (bf16[64,1152]{1,0:T(8,128)(2,1)S(1)}, bf16[64,1152]{1,0:T(8,128)(2,1)S(1)}, u32[]{:S(2)}, u32[]{:S(2)}) collective-permute-start(bf16[64,1152]{1,0:T(8,128)(2,1)S(1)} %get-tuple-element.30.refs_0_), channel_id=1, source_target_pairs={{0,17},{1,16},{2,19},{3,18},{4,21},{5,20},{6,23},{7,22},{8,14},{9,... | collective-permute-start | bytes 442376 | tf_op jit(solution)/shard_map/ppermute | solution.py:267
  16.3 7.6 %collective-permute-start.4 = (bf16[64,1152]{1,0:T(8,128)(2,1)S(1)}, bf16[64,1152]{1,0:T(8,128)(2,1)S(1)}, u32[]{:S(2)}, u32[]{:S(2)}) collective-permute-start(bf16[64,1152]{1,0:T(8,128)(2,1)S(1)} %get-tuple-element.30.refs_0_), channel_id=1, source_target_pairs={{0,16},{1,17},{2,18},{3,19},{4,20},{5,21},{6,22},{7,23},{8,12},{9,... | collective-permute-start | bytes 442376 | tf_op jit(solution)/shard_map/ppermute | solution.py:267
  16.3 7.6 %collective-permute-start.3 = (bf16[64,1152]{1,0:T(8,128)(2,1)S(1)}, bf16[64,1152]{1,0:T(8,128)(2,1)S(1)}, u32[]{:S(2)}, u32[]{:S(2)}) collective-permute-start(bf16[64,1152]{1,0:T(8,128)(2,1)S(1)} %get-tuple-element.30.refs_0_), channel_id=1, source_target_pairs={{0,1},{1,0},{2,3},{3,2},{4,5},{5,4},{6,7},{7,6},{8,10},{9,11},{10,... | collective-permute-start | bytes 442376 | tf_op jit(solution)/shard_map/ppermute | solution.py:267
  16.9 9.5 %slice-start = ((s8[8388608]{0:T(1024)(128)(4,1)}), s8[4194304]{0:T(1024)(128)(4,1)S(1)}, s32[]{:S(2)}) async-start(s8[8388608]{0:T(1024)(128)(4,1)} %bitcast.3), calls=%async_computation | async-start | bytes 8388608
  16.9 8.0 %collective-permute-start.9 = (bf16[64,1024]{1,0:T(8,128)(2,1)S(1)}, bf16[64,1024]{1,0:T(8,128)(2,1)S(1)}, u32[]{:S(2)}, u32[]{:S(2)}) collective-permute-start(bf16[64,1024]{1,0:T(8,128)(2,1)S(1)} %get-tuple-element.35.refs_0_), channel_id=1, source_target_pairs={{0,17},{1,16},{2,19},{3,18},{4,21},{5,20},{6,23},{7,22},{8,14},{9,... | collective-permute-start | bytes 393224 | tf_op jit(solution)/shard_map/ppermute | solution.py:267
  19.8 5.9 %collective-permute-start.8 = (bf16[64,1024]{1,0:T(8,128)(2,1)S(1)}, bf16[64,1024]{1,0:T(8,128)(2,1)S(1)}, u32[]{:S(2)}, u32[]{:S(2)}) collective-permute-start(bf16[64,1024]{1,0:T(8,128)(2,1)S(1)} %get-tuple-element.35.refs_0_), channel_id=1, source_target_pairs={{0,16},{1,17},{2,18},{3,19},{4,20},{5,21},{6,22},{7,23},{8,12},{9,... | collective-permute-start | bytes 393224 | tf_op jit(solution)/shard_map/ppermute | solution.py:267
  19.8 5.9 %collective-permute-start.7 = (bf16[64,1024]{1,0:T(8,128)(2,1)S(1)}, bf16[64,1024]{1,0:T(8,128)(2,1)S(1)}, u32[]{:S(2)}, u32[]{:S(2)}) collective-permute-start(bf16[64,1024]{1,0:T(8,128)(2,1)S(1)} %get-tuple-element.35.refs_0_), channel_id=1, source_target_pairs={{0,1},{1,0},{2,3},{3,2},{4,5},{5,4},{6,7},{7,6},{8,10},{9,11},{10,... | collective-permute-start | bytes 393224 | tf_op jit(solution)/shard_map/ppermute | solution.py:267
  23.9 2.5 %slice-start.1 = ((s8[8388608]{0:T(1024)(128)(4,1)}), s8[4194304]{0:T(1024)(128)(4,1)S(1)}, s32[]{:S(2)}) async-start(s8[8388608]{0:T(1024)(128)(4,1)} %bitcast.3), calls=%async_computation.1 | async-start | bytes 8388608
  24.8 1.6 %collective-permute-start.6 = (bf16[128,1152]{1,0:T(8,128)(2,1)S(1)}, bf16[128,1152]{1,0:T(8,128)(2,1)S(1)}, u32[]{:S(2)}, u32[]{:S(2)}) collective-permute-start(bf16[128,1152]{1,0:T(8,128)(2,1)S(1)} %get-tuple-element.34), channel_id=1, source_target_pairs={{0,8},{8,0},{16,24},{24,16},{1,9},{9,1},{17,25},{25,17},{2,10},{10... | collective-permute-start | bytes 884744 | tf_op jit(solution)/shard_map/ppermute | solution.py:270
  26.0 1.6 %collective-permute-start.10 = (bf16[128,1024]{1,0:T(8,128)(2,1)S(1)}, bf16[128,1024]{1,0:T(8,128)(2,1)S(1)}, u32[]{:S(2)}, u32[]{:S(2)}) collective-permute-start(bf16[128,1024]{1,0:T(8,128)(2,1)S(1)} %get-tuple-element.37), channel_id=1, source_target_pairs={{0,8},{8,0},{16,24},{24,16},{1,9},{9,1},{17,25},{25,17},{2,10},{10... | collective-permute-start | bytes 786440 | tf_op jit(solution)/shard_map/ppermute | solution.py:270
  28.6 22.2 %copy-start.1 = (f32[16]{0:T(128)S(1)}, f32[16]{0:T(128)}, u32[]{:S(2)}) copy-start(f32[16]{0:T(128)} %param.9) | copy-start | bytes 196
  29.6 1.6 %collective-permute-start.15 = (bf16[128,1024]{1,0:T(8,128)(2,1)S(1)}, bf16[128,1024]{1,0:T(8,128)(2,1)S(1)}, u32[]{:S(2)}, u32[]{:S(2)}) collective-permute-start(bf16[128,1024]{1,0:T(8,128)(2,1)S(1)} %get-tuple-element.46), channel_id=1, source_target_pairs={{0,8},{8,0},{16,24},{24,16},{1,9},{9,1},{17,25},{25,17},{2,10},{10... | collective-permute-start | bytes 786440 | tf_op jit(solution)/shard_map/ppermute | solution.py:270
  30.6 4.8 %collective-permute-start.11 = (bf16[128,1024]{1,0:T(8,128)(2,1)S(1)}, bf16[128,1024]{1,0:T(8,128)(2,1)S(1)}, u32[]{:S(2)}, u32[]{:S(2)}) collective-permute-start(bf16[128,1024]{1,0:T(8,128)(2,1)S(1)} %get-tuple-element.40), channel_id=1, source_target_pairs={{0,8},{8,0},{16,24},{24,16},{1,9},{9,1},{17,25},{25,17},{2,10},{10... | collective-permute-start | bytes 786440 | tf_op jit(solution)/shard_map/ppermute | solution.py:270
  31.6 6.7 %collective-permute-start.16 = (bf16[64,1024]{1,0:T(8,128)(2,1)S(1)}, bf16[64,1024]{1,0:T(8,128)(2,1)S(1)}, u32[]{:S(2)}, u32[]{:S(2)}) collective-permute-start(bf16[64,1024]{1,0:T(8,128)(2,1)S(1)} %get-tuple-element.48), channel_id=1, source_target_pairs={{0,17},{1,16},{2,19},{3,18},{4,21},{5,20},{6,23},{7,22},{8,14},{9,... | collective-permute-start | bytes 393224 | tf_op jit(solution)/shard_map/ppermute | solution.py:267
  34.3 5.2 %collective-permute-start.17 = (bf16[64,1024]{1,0:T(8,128)(2,1)S(1)}, bf16[64,1024]{1,0:T(8,128)(2,1)S(1)}, u32[]{:S(2)}, u32[]{:S(2)}) collective-permute-start(bf16[64,1024]{1,0:T(8,128)(2,1)S(1)} %get-tuple-element.49), channel_id=1, source_target_pairs={{0,16},{1,17},{2,18},{3,19},{4,20},{5,21},{6,22},{7,23},{8,12},{9,... | collective-permute-start | bytes 393224 | tf_op jit(solution)/shard_map/ppermute | solution.py:267
  34.3 5.6 %collective-permute-start.18 = (bf16[64,1024]{1,0:T(8,128)(2,1)S(1)}, bf16[64,1024]{1,0:T(8,128)(2,1)S(1)}, u32[]{:S(2)}, u32[]{:S(2)}) collective-permute-start(bf16[64,1024]{1,0:T(8,128)(2,1)S(1)} %get-tuple-element.50), channel_id=1, source_target_pairs={{0,1},{1,0},{2,3},{3,2},{4,5},{5,4},{6,7},{7,6},{8,10},{9,11},{10,... | collective-permute-start | bytes 393224 | tf_op jit(solution)/shard_map/ppermute | solution.py:267
  36.0 6.2 %collective-permute-start.12 = (bf16[64,1024]{1,0:T(8,128)(2,1)S(1)}, bf16[64,1024]{1,0:T(8,128)(2,1)S(1)}, u32[]{:S(2)}, u32[]{:S(2)}) collective-permute-start(bf16[64,1024]{1,0:T(8,128)(2,1)S(1)} %get-tuple-element.42), channel_id=1, source_target_pairs={{0,17},{1,16},{2,19},{3,18},{4,21},{5,20},{6,23},{7,22},{8,14},{9,... | collective-permute-start | bytes 393224 | tf_op jit(solution)/shard_map/ppermute | solution.py:267
  38.3 5.2 %collective-permute-start.13 = (bf16[64,1024]{1,0:T(8,128)(2,1)S(1)}, bf16[64,1024]{1,0:T(8,128)(2,1)S(1)}, u32[]{:S(2)}, u32[]{:S(2)}) collective-permute-start(bf16[64,1024]{1,0:T(8,128)(2,1)S(1)} %get-tuple-element.43), channel_id=1, source_target_pairs={{0,16},{1,17},{2,18},{3,19},{4,20},{5,21},{6,22},{7,23},{8,12},{9,... | collective-permute-start | bytes 393224 | tf_op jit(solution)/shard_map/ppermute | solution.py:267
  38.3 5.6 %collective-permute-start.14 = (bf16[64,1024]{1,0:T(8,128)(2,1)S(1)}, bf16[64,1024]{1,0:T(8,128)(2,1)S(1)}, u32[]{:S(2)}, u32[]{:S(2)}) collective-permute-start(bf16[64,1024]{1,0:T(8,128)(2,1)S(1)} %get-tuple-element.44), channel_id=1, source_target_pairs={{0,1},{1,0},{2,3},{3,2},{4,5},{5,4},{6,7},{7,6},{8,10},{9,11},{10,... | collective-permute-start | bytes 393224 | tf_op jit(solution)/shard_map/ppermute | solution.py:267
  44.0 6.1 %collective-permute-start.19 = (bf16[16,2048]{1,0:T(8,128)(2,1)S(1)}, bf16[16,2048]{1,0:T(8,128)(2,1)S(1)}, u32[]{:S(2)}, u32[]{:S(2)}) collective-permute-start(bf16[16,2048]{1,0:T(8,128)(2,1)S(1)} %get-tuple-element.52), channel_id=1, source_target_pairs={{0,6},{1,7},{2,4},{3,5},{4,2},{5,3},{6,0},{7,1},{8,25},{9,24},{10,... | collective-permute-start | bytes 196616 | tf_op jit(solution)/shard_map/ppermute | solution.py:267
  44.1 6.1 %collective-permute-start.20 = (bf16[16,2048]{1,0:T(8,128)(2,1)S(1)}, bf16[16,2048]{1,0:T(8,128)(2,1)S(1)}, u32[]{:S(2)}, u32[]{:S(2)}) collective-permute-start(bf16[16,2048]{1,0:T(8,128)(2,1)S(1)} %get-tuple-element.53), channel_id=1, source_target_pairs={{0,4},{1,5},{2,6},{3,7},{4,0},{5,1},{6,2},{7,3},{8,24},{9,25},{10,... | collective-permute-start | bytes 196616 | tf_op jit(solution)/shard_map/ppermute | solution.py:267
  45.1 5.7 %collective-permute-start.21 = (bf16[16,2048]{1,0:T(8,128)(2,1)S(1)}, bf16[16,2048]{1,0:T(8,128)(2,1)S(1)}, u32[]{:S(2)}, u32[]{:S(2)}) collective-permute-start(bf16[16,2048]{1,0:T(8,128)(2,1)S(1)} %get-tuple-element.54), channel_id=1, source_target_pairs={{0,2},{1,3},{2,0},{3,1},{4,6},{5,7},{6,4},{7,5},{8,9},{9,8},{10,11... | collective-permute-start | bytes 196616 | tf_op jit(solution)/shard_map/ppermute | solution.py:267

commit v2 on v1

--- a/solution.py
+++ b/solution.py
@@ -250,7 +250,7 @@
     widths = [model // 2, model // 2]
     chunks = len(widths)
     starts = [sum(widths[:i]) for i in range(chunks)]
-    step = min(256, units)
+    step = min(512, units)
 
 
     mixed = far == blocks
@@ -343,7 +343,7 @@
     for chunk in reversed(range(chunks)):
         width = widths[chunk]
         own, other = call(
-            functools.partial(down_kernel, min(256, width), starts[chunk], width),
+            functools.partial(down_kernel, min(512, width), starts[chunk], width),
             f"down_{chunk}",
             [((half, width), BF16)] * 2,
             [*slots[0], hidden, down_held],

time: 52.6 us -> 52.4 us (level)
  no operation moved by 1% of the time
where the time goes in v2:
time: 52.4 us; the launch traced here: 51.6 us
  starting transfers between devices  26.8 us (51%)
  waiting for transfers between devices  12.8 us (24%)
  Pallas kernels  10.3 us (20%)
  local copies, waits for them, and re-layouts  0.86 us (2%)
  other arithmetic  0.68 us (1%)
    ppermute x18, starting transfers between devices, exchange(): return lax.ppermute(value, ('group', 'inner'), pairs)  26 us
    ppermute x18, waiting for transfers between devices, exchange(): return lax.ppermute(value, ('group', 'inner'), pairs)  12.1 us
    pallas_call x13, Pallas kernels, call(): pl.pallas_call(kernel, out_shape=shapes, in_specs=specs or [VMEM_SPEC] *...  10.3 us
  transfers between devices with their start and end apart: 22, of which 12 were waited for; matrix products, arithmetic and copies ran while one was open for 0% of the time, Pallas kernels for 14%

profile of v2, /device:TPU:0, one launch (start us, length us, event | category | flops | bytes accessed | tf_op | source)
XLA Modules:
  0.0 51.6 jit_solution(15825338875925285465)
XLA Ops:
  0.0 0.7 %add_bitcast_fusion.expert_ref = s32[1,16]{1,0:T(1,128)S(1)} fusion(s32[16,1]{0,1:T(1,128)} %param.8, s32[16,1]{0,1:T(1,128)} %param.7), kind=kLoop, calls=%fused_computation | loop fusion | flops 32 | bytes 192 | tf_op jit(solution)/shard_map/reshape | solution.py:278
  0.7 0.0 copy-start
  0.7 0.8 %copy-done = bf16[16,2048]{1,0:T(8,128)(2,1)S(1)} copy-done((bf16[16,2048]{1,0:T(8,128)(2,1)S(1)}, bf16[16,2048]{1,0:T(8,128)(2,1)}, u32[]{:S(2)}) %copy-start) | copy-done | bytes 65560
  1.5 0.2 tag_rows.1.refs_0_
  1.7 5.1 %collective-permute-start.2 = (bf16[16,2176]{1,0:T(8,128)(2,1)S(1)}, bf16[16,2176]{1,0:T(8,128)(2,1)S(1)}, u32[]{:S(2)}, u32[]{:S(2)}) collective-permute-start(bf16[16,2176]{1,0:T(8,128)(2,1)S(1)} %tag_rows.1.refs_0_), channel_id=1, source_target_pairs={{0,6},{1,7},{2,4},{3,5},{4,2},{5,3},{6,0},{7,1},{8,25},{9,24},{10,... | collective-permute-start | bytes 208904 | tf_op jit(solution)/shard_map/ppermute | solution.py:267
  6.8 0.0 collective-permute-start.1
  6.8 0.6 %collective-permute-start = (bf16[16,2176]{1,0:T(8,128)(2,1)S(1)}, bf16[16,2176]{1,0:T(8,128)(2,1)S(1)}, u32[]{:S(2)}, u32[]{:S(2)}) collective-permute-start(bf16[16,2176]{1,0:T(8,128)(2,1)S(1)} %tag_rows.1.refs_0_), channel_id=1, source_target_pairs={{0,2},{1,3},{2,0},{3,1},{4,6},{5,7},{6,4},{7,5},{8,9},{9,8},{10,11... | collective-permute-start | bytes 208904 | tf_op jit(solution)/shard_map/ppermute | solution.py:267
  7.4 1.8 %collective-permute-done.2.refs_3_ = bf16[16,2176]{1,0:T(8,128)(2,1)S(1)} collective-permute-done((bf16[16,2176]{1,0:T(8,128)(2,1)S(1)}, bf16[16,2176]{1,0:T(8,128)(2,1)S(1)}, u32[]{:S(2)}, u32[]{:S(2)}) %collective-permute-start.2) | collective-permute-done | bytes 69664 | tf_op jit(solution)/shard_map/ppermute | solution.py:267
  9.2 2.8 %collective-permute-done.1.refs_2_ = bf16[16,2176]{1,0:T(8,128)(2,1)S(1)} collective-permute-done((bf16[16,2176]{1,0:T(8,128)(2,1)S(1)}, bf16[16,2176]{1,0:T(8,128)(2,1)S(1)}, u32[]{:S(2)}, u32[]{:S(2)}) %collective-permute-start.1) | collective-permute-done | bytes 69664 | tf_op jit(solution)/shard_map/ppermute | solution.py:267
  12.0 0.0 collective-permute-done.refs_1_
  12.0 4.3 %collective-permute-start.5 = (bf16[64,1152]{1,0:T(8,128)(2,1)S(1)}, bf16[64,1152]{1,0:T(8,128)(2,1)S(1)}, u32[]{:S(2)}, u32[]{:S(2)}) collective-permute-start(bf16[64,1152]{1,0:T(8,128)(2,1)S(1)} %get-tuple-element.30.refs_0_), channel_id=1, source_target_pairs={{0,17},{1,16},{2,19},{3,18},{4,21},{5,20},{6,23},{7,22},{8,14},{9,... | collective-permute-start | bytes 442376 | tf_op jit(solution)/shard_map/ppermute | solution.py:267
  16.3 0.0 collective-permute-start.4
  16.3 0.6 %collective-permute-start.3 = (bf16[64,1152]{1,0:T(8,128)(2,1)S(1)}, bf16[64,1152]{1,0:T(8,128)(2,1)S(1)}, u32[]{:S(2)}, u32[]{:S(2)}) collective-permute-start(bf16[64,1152]{1,0:T(8,128)(2,1)S(1)} %get-tuple-element.30.refs_0_), channel_id=1, source_target_pairs={{0,1},{1,0},{2,3},{3,2},{4,5},{5,4},{6,7},{7,6},{8,10},{9,11},{10,... | collective-permute-start | bytes 442376 | tf_op jit(solution)/shard_map/ppermute | solution.py:267
  16.9 2.8 %collective-permute-start.9 = (bf16[64,1024]{1,0:T(8,128)(2,1)S(1)}, bf16[64,1024]{1,0:T(8,128)(2,1)S(1)}, u32[]{:S(2)}, u32[]{:S(2)}) collective-permute-start(bf16[64,1024]{1,0:T(8,128)(2,1)S(1)} %get-tuple-element.35.refs_0_), channel_id=1, source_target_pairs={{0,17},{1,16},{2,19},{3,18},{4,21},{5,20},{6,23},{7,22},{8,14},{9,... | collective-permute-start | bytes 393224 | tf_op jit(solution)/shard_map/ppermute | solution.py:267
  19.8 0.0 collective-permute-start.8
  19.8 0.0 collective-permute-done.5.after_ref.refs_3_
  19.8 0.6 %collective-permute-start.7 = (bf16[64,1024]{1,0:T(8,128)(2,1)S(1)}, bf16[64,1024]{1,0:T(8,128)(2,1)S(1)}, u32[]{:S(2)}, u32[]{:S(2)}) collective-permute-start(bf16[64,1024]{1,0:T(8,128)(2,1)S(1)} %get-tuple-element.35.refs_0_), channel_id=1, source_target_pairs={{0,1},{1,0},{2,3},{3,2},{4,5},{5,4},{6,7},{7,6},{8,10},{9,11},{10,... | collective-permute-start | bytes 393224 | tf_op jit(solution)/shard_map/ppermute | solution.py:267
  20.4 3.5 %load_down.1 = (bf16[2,1024,2048]{2,1,0:T(8,128)(2,1)S(1)}, f32[8,128]{1,0:T(8,128)S(1)}) custom-call(bf16[64,1152]{1,0:T(8,128)(2,1)S(1)} %collective-permute-done.5.after_ref.refs_3_, bf16[2,1024,2048]{2,1,0:T(8,128)(2,1)} %weight_ref.1), custom_call_target="tpu_custom_call" | custom-call | bytes 16777216 | tf_op jit(solution)/shard_map/load_down/pallas_call | solution.py:23
  23.9 0.0 collective-permute-done.4.refs_2_
  23.9 0.0 collective-permute-done.3.refs_1_
  23.9 0.0 slice-start.1
  24.0 0.9 %pack_0.1 = (bf16[128,1152]{1,0:T(8,128)(2,1)S(1)}, bf16[128,1152]{1,0:T(8,128)(2,1)S(1)}, bf16[256,256]{1,0:T(8,128)(2,1)S(1)}) custom-call(bf16[64,1152]{1,0:T(8,128)(2,1)S(1)} %get-tuple-element.30.refs_0_, bf16[64,1152]{1,0:T(8,128)(2,1)S(1)} %collective-permute-done.3.refs_1_, bf16[64,1152]{1,0:T(8,128)(2,1)S(1)} %collective-permute-done.4.refs_2_, ...), custom_call_target="tpu_custom_call" | custom-call | flops 1500000000 | tf_op jit(solution)/shard_map/pack_0/pallas_call | solution.py:23
  24.8 0.1 collective-permute-start.6
  24.9 0.0 collective-permute-done.9.refs_3_
  24.9 0.8 %collective-permute-done.8.refs_2_ = bf16[64,1024]{1,0:T(8,128)(2,1)S(1)} collective-permute-done((bf16[64,1024]{1,0:T(8,128)(2,1)S(1)}, bf16[64,1024]{1,0:T(8,128)(2,1)S(1)}, u32[]{:S(2)}, u32[]{:S(2)}) %collective-permute-start.8) | collective-permute-done | bytes 131104 | tf_op jit(solution)/shard_map/ppermute | solution.py:267
  25.7 0.0 collective-permute-done.7.refs_1_
  25.7 0.3 pack_1.1
  26.0 0.1 collective-permute-start.10
  26.1 0.4 collective-permute-done.6.other_ref.other_tag
  26.5 0.0 slice-done
  26.5 0.0 slice-done.1
  26.5 0.9 %up_first.1.acc_ref = f32[256,1024]{1,0:T(8,128)S(1)} custom-call(bf16[128,1152]{1,0:T(8,128)(2,1)S(1)} %get-tuple-element.33.own_ref.own_tag, bf16[128,1152]{1,0:T(8,128)(2,1)S(1)} %collective-permute-done.6.other_ref.other_tag, bf16[2,2048,1024]{2,1,0:T(8,128)(2,1)S(1)} %bitcast.4), custom_call_target="tpu_custom_call" | custom-call | flops 1073741824 | tf_op jit(solution)/shard_map/up_first/pallas_call | solution.py:23
  27.4 0.3 collective-permute-done.10.other_ref
  27.6 1.0 %up_last.1.hidden_ref = bf16[256,1024]{1,0:T(8,128)(2,1)S(1)} custom-call(bf16[128,1152]{1,0:T(8,128)(2,1)S(1)} %get-tuple-element.33.own_ref.own_tag, bf16[128,1152]{1,0:T(8,128)(2,1)S(1)} %collective-permute-done.6.other_ref.other_tag, bf16[128,1024]{1,0:T(8,128)(2,1)S(1)} %get-tuple-element.36.own_ref, ...), custom_call_target="tpu_custom_call" | custom-call | flops 1073741824 | tf_op jit(solution)/shard_map/up_last/pallas_call | solution.py:23
  28.6 0.0 copy-start.1
  28.6 0.9 %down_1.1 = (bf16[128,1024]{1,0:T(8,128)(2,1)S(1)}, bf16[128,1024]{1,0:T(8,128)(2,1)S(1)}) custom-call(bf16[128,1152]{1,0:T(8,128)(2,1)S(1)} %get-tuple-element.33.own_ref.own_tag, bf16[128,1152]{1,0:T(8,128)(2,1)S(1)} %collective-permute-done.6.other_ref.other_tag, bf16[256,1024]{1,0:T(8,128)(2,1)S(1)} %up_last.1.hidden_ref, ...), custom_call_target="tpu_custom_call" | custom-call | flops 1073741824 | tf_op jit(solution)/shard_map/down_1/pallas_call | solution.py:23
  29.5 0.2 collective-permute-start.15
  29.7 0.9 %down_0.1 = (bf16[128,1024]{1,0:T(8,128)(2,1)S(1)}, bf16[128,1024]{1,0:T(8,128)(2,1)S(1)}) custom-call(bf16[128,1152]{1,0:T(8,128)(2,1)S(1)} %get-tuple-element.33.own_ref.own_tag, bf16[128,1152]{1,0:T(8,128)(2,1)S(1)} %collective-permute-done.6.other_ref.other_tag, bf16[256,1024]{1,0:T(8,128)(2,1)S(1)} %up_last.1.hidden_ref, ...), custom_call_target="tpu_custom_call" | custom-call | flops 1073741824 | tf_op jit(solution)/shard_map/down_0/pallas_call | solution.py:23
  30.6 0.4 collective-permute-start.11
  31.1 0.1 collective-permute-done.15.other_ref
  31.1 0.5 unpack_slots.3
  31.6 2.7 %collective-permute-start.16 = (bf16[64,1024]{1,0:T(8,128)(2,1)S(1)}, bf16[64,1024]{1,0:T(8,128)(2,1)S(1)}, u32[]{:S(2)}, u32[]{:S(2)}) collective-permute-start(bf16[64,1024]{1,0:T(8,128)(2,1)S(1)} %get-tuple-element.48), channel_id=1, source_target_pairs={{0,17},{1,16},{2,19},{3,18},{4,21},{5,20},{6,23},{7,22},{8,14},{9,... | collective-permute-start | bytes 393224 | tf_op jit(solution)/shard_map/ppermute | solution.py:267
  34.3 0.0 collective-permute-start.17
  34.3 1.2 %collective-permute-start.18 = (bf16[64,1024]{1,0:T(8,128)(2,1)S(1)}, bf16[64,1024]{1,0:T(8,128)(2,1)S(1)}, u32[]{:S(2)}, u32[]{:S(2)}) collective-permute-start(bf16[64,1024]{1,0:T(8,128)(2,1)S(1)} %get-tuple-element.50), channel_id=1, source_target_pairs={{0,1},{1,0},{2,3},{3,2},{4,5},{5,4},{6,7},{7,6},{8,10},{9,11},{10,... | collective-permute-start | bytes 393224 | tf_op jit(solution)/shard_map/ppermute | solution.py:267
  35.5 0.0 collective-permute-done.11.other_ref
  35.5 0.5 unpack_slots.2
  36.0 2.4 %collective-permute-start.12 = (bf16[64,1024]{1,0:T(8,128)(2,1)S(1)}, bf16[64,1024]{1,0:T(8,128)(2,1)S(1)}, u32[]{:S(2)}, u32[]{:S(2)}) collective-permute-start(bf16[64,1024]{1,0:T(8,128)(2,1)S(1)} %get-tuple-element.42), channel_id=1, source_target_pairs={{0,17},{1,16},{2,19},{3,18},{4,21},{5,20},{6,23},{7,22},{8,14},{9,... | collective-permute-start | bytes 393224 | tf_op jit(solution)/shard_map/ppermute | solution.py:267
  38.3 0.0 collective-permute-start.13
  38.3 0.0 collective-permute-done.16.refs_5_
  38.3 1.2 %collective-permute-start.14 = (bf16[64,1024]{1,0:T(8,128)(2,1)S(1)}, bf16[64,1024]{1,0:T(8,128)(2,1)S(1)}, u32[]{:S(2)}, u32[]{:S(2)}) collective-permute-start(bf16[64,1024]{1,0:T(8,128)(2,1)S(1)} %get-tuple-element.44), channel_id=1, source_target_pairs={{0,1},{1,0},{2,3},{3,2},{4,5},{5,4},{6,7},{7,6},{8,10},{9,11},{10,... | collective-permute-start | bytes 393224 | tf_op jit(solution)/shard_map/ppermute | solution.py:267
  39.5 0.0 collective-permute-done.17.refs_6_
  39.5 0.3 collective-permute-done.18.refs_7_
  39.9 2.3 %collective-permute-done.12.refs_1_ = bf16[64,1024]{1,0:T(8,128)(2,1)S(1)} collective-permute-done((bf16[64,1024]{1,0:T(8,128)(2,1)S(1)}, bf16[64,1024]{1,0:T(8,128)(2,1)S(1)}, u32[]{:S(2)}, u32[]{:S(2)}) %collective-permute-start.12) | collective-permute-done | bytes 131104 | tf_op jit(solution)/shard_map/ppermute | solution.py:267
  42.1 1.4 %collective-permute-done.13.refs_2_ = bf16[64,1024]{1,0:T(8,128)(2,1)S(1)} collective-permute-done((bf16[64,1024]{1,0:T(8,128)(2,1)S(1)}, bf16[64,1024]{1,0:T(8,128)(2,1)S(1)}, u32[]{:S(2)}, u32[]{:S(2)}) %collective-permute-start.13) | collective-permute-done | bytes 131104 | tf_op jit(solution)/shard_map/ppermute | solution.py:267
  43.5 0.4 collective-permute-done.14.refs_3_
  43.9 0.1 add_plane.1
  44.0 0.1 collective-permute-start.19
  44.1 1.0 %collective-permute-start.20 = (bf16[16,2048]{1,0:T(8,128)(2,1)S(1)}, bf16[16,2048]{1,0:T(8,128)(2,1)S(1)}, u32[]{:S(2)}, u32[]{:S(2)}) collective-permute-start(bf16[16,2048]{1,0:T(8,128)(2,1)S(1)} %get-tuple-element.53), channel_id=1, source_target_pairs={{0,4},{1,5},{2,6},{3,7},{4,0},{5,1},{6,2},{7,3},{8,24},{9,25},{10,... | collective-permute-start | bytes 196616 | tf_op jit(solution)/shard_map/ppermute | solution.py:267
  45.1 3.4 %collective-permute-start.21 = (bf16[16,2048]{1,0:T(8,128)(2,1)S(1)}, bf16[16,2048]{1,0:T(8,128)(2,1)S(1)}, u32[]{:S(2)}, u32[]{:S(2)}) collective-permute-start(bf16[16,2048]{1,0:T(8,128)(2,1)S(1)} %get-tuple-element.54), channel_id=1, source_target_pairs={{0,2},{1,3},{2,0},{3,1},{4,6},{5,7},{6,4},{7,5},{8,9},{9,8},{10,11... | collective-permute-start | bytes 196616 | tf_op jit(solution)/shard_map/ppermute | solution.py:267
  48.5 1.7 %collective-permute-done.19.refs_1_ = bf16[16,2048]{1,0:T(8,128)(2,1)S(1)} collective-permute-done((bf16[16,2048]{1,0:T(8,128)(2,1)S(1)}, bf16[16,2048]{1,0:T(8,128)(2,1)S(1)}, u32[]{:S(2)}, u32[]{:S(2)}) %collective-permute-start.19) | collective-permute-done | bytes 65568 | tf_op jit(solution)/shard_map/ppermute | solution.py:267
  50.2 0.0 collective-permute-done.20.refs_2_
  50.2 0.7 %collective-permute-done.21.refs_3_ = bf16[16,2048]{1,0:T(8,128)(2,1)S(1)} collective-permute-done((bf16[16,2048]{1,0:T(8,128)(2,1)S(1)}, bf16[16,2048]{1,0:T(8,128)(2,1)S(1)}, u32[]{:S(2)}, u32[]{:S(2)}) %collective-permute-start.21) | collective-permute-done | bytes 65568 | tf_op jit(solution)/shard_map/ppermute | solution.py:267
  50.9 0.0 copy-done.1
  50.9 0.7 %finish.1 = bf16[16,2048]{1,0:T(8,128)(2,1)} custom-call(f32[1,16]{1,0:T(1,128)S(1)} %bitcast.5, bf16[16,2048]{1,0:T(8,128)(2,1)S(1)} %get-tuple-element.51.refs_0_, bf16[16,2048]{1,0:T(8,128)(2,1)S(1)} %collective-permute-done.19.refs_1_, bf16[16,2048]{1,0:T(8,128)(2,1)S(1)} %collective-permute-done.20.refs_2_, ...), custom_call_target="tpu_custom_call" | custom-call | tf_op jit(solution)/shard_map/finish/pallas_call | solution.py:23
  (3 shorter events, 0.0 us)
Async XLA Ops:
  0.7 0.8 %copy-start = (bf16[16,2048]{1,0:T(8,128)(2,1)S(1)}, bf16[16,2048]{1,0:T(8,128)(2,1)}, u32[]{:S(2)}) copy-start(bf16[16,2048]{1,0:T(8,128)(2,1)} %rows_ref.1) | copy-start | bytes 196612
  1.7 7.5 %collective-permute-start.2 = (bf16[16,2176]{1,0:T(8,128)(2,1)S(1)}, bf16[16,2176]{1,0:T(8,128)(2,1)S(1)}, u32[]{:S(2)}, u32[]{:S(2)}) collective-permute-start(bf16[16,2176]{1,0:T(8,128)(2,1)S(1)} %tag_rows.1.refs_0_), channel_id=1, source_target_pairs={{0,6},{1,7},{2,4},{3,5},{4,2},{5,3},{6,0},{7,1},{8,25},{9,24},{10,... | collective-permute-start | bytes 208904 | tf_op jit(solution)/shard_map/ppermute | solution.py:267
  6.8 5.2 %collective-permute-start.1 = (bf16[16,2176]{1,0:T(8,128)(2,1)S(1)}, bf16[16,2176]{1,0:T(8,128)(2,1)S(1)}, u32[]{:S(2)}, u32[]{:S(2)}) collective-permute-start(bf16[16,2176]{1,0:T(8,128)(2,1)S(1)} %tag_rows.1.refs_0_), channel_id=1, source_target_pairs={{0,4},{1,5},{2,6},{3,7},{4,0},{5,1},{6,2},{7,3},{8,24},{9,25},{10,... | collective-permute-start | bytes 208904 | tf_op jit(solution)/shard_map/ppermute | solution.py:267
  6.8 5.2 %collective-permute-start = (bf16[16,2176]{1,0:T(8,128)(2,1)S(1)}, bf16[16,2176]{1,0:T(8,128)(2,1)S(1)}, u32[]{:S(2)}, u32[]{:S(2)}) collective-permute-start(bf16[16,2176]{1,0:T(8,128)(2,1)S(1)} %tag_rows.1.refs_0_), channel_id=1, source_target_pairs={{0,2},{1,3},{2,0},{3,1},{4,6},{5,7},{6,4},{7,5},{8,9},{9,8},{10,11... | collective-permute-start | bytes 208904 | tf_op jit(solution)/shard_map/ppermute | solution.py:267
  12.0 7.8 %collective-permute-start.5 = (bf16[64,1152]{1,0:T(8,128)(2,1)S(1)}, bf16[64,1152]{1,0:T(8,128)(2,1)S(1)}, u32[]{:S(2)}, u32[]{:S(2)}) collective-permute-start(bf16[64,1152]{1,0:T(8,128)(2,1)S(1)} %get-tuple-element.30.refs_0_), channel_id=1, source_target_pairs={{0,17},{1,16},{2,19},{3,18},{4,21},{5,20},{6,23},{7,22},{8,14},{9,... | collective-permute-start | bytes 442376 | tf_op jit(solution)/shard_map/ppermute | solution.py:267
  16.3 7.6 %collective-permute-start.4 = (bf16[64,1152]{1,0:T(8,128)(2,1)S(1)}, bf16[64,1152]{1,0:T(8,128)(2,1)S(1)}, u32[]{:S(2)}, u32[]{:S(2)}) collective-permute-start(bf16[64,1152]{1,0:T(8,128)(2,1)S(1)} %get-tuple-element.30.refs_0_), channel_id=1, source_target_pairs={{0,16},{1,17},{2,18},{3,19},{4,20},{5,21},{6,22},{7,23},{8,12},{9,... | collective-permute-start | bytes 442376 | tf_op jit(solution)/shard_map/ppermute | solution.py:267
  16.3 7.6 %collective-permute-start.3 = (bf16[64,1152]{1,0:T(8,128)(2,1)S(1)}, bf16[64,1152]{1,0:T(8,128)(2,1)S(1)}, u32[]{:S(2)}, u32[]{:S(2)}) collective-permute-start(bf16[64,1152]{1,0:T(8,128)(2,1)S(1)} %get-tuple-element.30.refs_0_), channel_id=1, source_target_pairs={{0,1},{1,0},{2,3},{3,2},{4,5},{5,4},{6,7},{7,6},{8,10},{9,11},{10,... | collective-permute-start | bytes 442376 | tf_op jit(solution)/shard_map/ppermute | solution.py:267
  16.9 9.5 %slice-start = ((s8[8388608]{0:T(1024)(128)(4,1)}), s8[4194304]{0:T(1024)(128)(4,1)S(1)}, s32[]{:S(2)}) async-start(s8[8388608]{0:T(1024)(128)(4,1)} %bitcast.3), calls=%async_computation | async-start | bytes 8388608
  16.9 8.0 %collective-permute-start.9 = (bf16[64,1024]{1,0:T(8,128)(2,1)S(1)}, bf16[64,1024]{1,0:T(8,128)(2,1)S(1)}, u32[]{:S(2)}, u32[]{:S(2)}) collective-permute-start(bf16[64,1024]{1,0:T(8,128)(2,1)S(1)} %get-tuple-element.35.refs_0_), channel_id=1, source_target_pairs={{0,17},{1,16},{2,19},{3,18},{4,21},{5,20},{6,23},{7,22},{8,14},{9,... | collective-permute-start | bytes 393224 | tf_op jit(solution)/shard_map/ppermute | solution.py:267
  19.8 5.9 %collective-permute-start.8 = (bf16[64,1024]{1,0:T(8,128)(2,1)S(1)}, bf16[64,1024]{1,0:T(8,128)(2,1)S(1)}, u32[]{:S(2)}, u32[]{:S(2)}) collective-permute-start(bf16[64,1024]{1,0:T(8,128)(2,1)S(1)} %get-tuple-element.35.refs_0_), channel_id=1, source_target_pairs={{0,16},{1,17},{2,18},{3,19},{4,20},{5,21},{6,22},{7,23},{8,12},{9,... | collective-permute-start | bytes 393224 | tf_op jit(solution)/shard_map/ppermute | solution.py:267
  19.8 5.9 %collective-permute-start.7 = (bf16[64,1024]{1,0:T(8,128)(2,1)S(1)}, bf16[64,1024]{1,0:T(8,128)(2,1)S(1)}, u32[]{:S(2)}, u32[]{:S(2)}) collective-permute-start(bf16[64,1024]{1,0:T(8,128)(2,1)S(1)} %get-tuple-element.35.refs_0_), channel_id=1, source_target_pairs={{0,1},{1,0},{2,3},{3,2},{4,5},{5,4},{6,7},{7,6},{8,10},{9,11},{10,... | collective-permute-start | bytes 393224 | tf_op jit(solution)/shard_map/ppermute | solution.py:267
  23.9 2.5 %slice-start.1 = ((s8[8388608]{0:T(1024)(128)(4,1)}), s8[4194304]{0:T(1024)(128)(4,1)S(1)}, s32[]{:S(2)}) async-start(s8[8388608]{0:T(1024)(128)(4,1)} %bitcast.3), calls=%async_computation.1 | async-start | bytes 8388608
  24.8 1.6 %collective-permute-start.6 = (bf16[128,1152]{1,0:T(8,128)(2,1)S(1)}, bf16[128,1152]{1,0:T(8,128)(2,1)S(1)}, u32[]{:S(2)}, u32[]{:S(2)}) collective-permute-start(bf16[128,1152]{1,0:T(8,128)(2,1)S(1)} %get-tuple-element.34), channel_id=1, source_target_pairs={{0,8},{8,0},{16,24},{24,16},{1,9},{9,1},{17,25},{25,17},{2,10},{10... | collective-permute-start | bytes 884744 | tf_op jit(solution)/shard_map/ppermute | solution.py:270
  26.0 1.6 %collective-permute-start.10 = (bf16[128,1024]{1,0:T(8,128)(2,1)S(1)}, bf16[128,1024]{1,0:T(8,128)(2,1)S(1)}, u32[]{:S(2)}, u32[]{:S(2)}) collective-permute-start(bf16[128,1024]{1,0:T(8,128)(2,1)S(1)} %get-tuple-element.37), channel_id=1, source_target_pairs={{0,8},{8,0},{16,24},{24,16},{1,9},{9,1},{17,25},{25,17},{2,10},{10... | collective-permute-start | bytes 786440 | tf_op jit(solution)/shard_map/ppermute | solution.py:270
  28.6 22.2 %copy-start.1 = (f32[16]{0:T(128)S(1)}, f32[16]{0:T(128)}, u32[]{:S(2)}) copy-start(f32[16]{0:T(128)} %param.9) | copy-start | bytes 196
  29.5 1.6 %collective-permute-start.15 = (bf16[128,1024]{1,0:T(8,128)(2,1)S(1)}, bf16[128,1024]{1,0:T(8,128)(2,1)S(1)}, u32[]{:S(2)}, u32[]{:S(2)}) collective-permute-start(bf16[128,1024]{1,0:T(8,128)(2,1)S(1)} %get-tuple-element.46), channel_id=1, source_target_pairs={{0,8},{8,0},{16,24},{24,16},{1,9},{9,1},{17,25},{25,17},{2,10},{10... | collective-permute-start | bytes 786440 | tf_op jit(solution)/shard_map/ppermute | solution.py:270
  30.6 4.9 %collective-permute-start.11 = (bf16[128,1024]{1,0:T(8,128)(2,1)S(1)}, bf16[128,1024]{1,0:T(8,128)(2,1)S(1)}, u32[]{:S(2)}, u32[]{:S(2)}) collective-permute-start(bf16[128,1024]{1,0:T(8,128)(2,1)S(1)} %get-tuple-element.40), channel_id=1, source_target_pairs={{0,8},{8,0},{16,24},{24,16},{1,9},{9,1},{17,25},{25,17},{2,10},{10... | collective-permute-start | bytes 786440 | tf_op jit(solution)/shard_map/ppermute | solution.py:270
  31.6 6.7 %collective-permute-start.16 = (bf16[64,1024]{1,0:T(8,128)(2,1)S(1)}, bf16[64,1024]{1,0:T(8,128)(2,1)S(1)}, u32[]{:S(2)}, u32[]{:S(2)}) collective-permute-start(bf16[64,1024]{1,0:T(8,128)(2,1)S(1)} %get-tuple-element.48), channel_id=1, source_target_pairs={{0,17},{1,16},{2,19},{3,18},{4,21},{5,20},{6,23},{7,22},{8,14},{9,... | collective-permute-start | bytes 393224 | tf_op jit(solution)/shard_map/ppermute | solution.py:267
  34.3 5.2 %collective-permute-start.17 = (bf16[64,1024]{1,0:T(8,128)(2,1)S(1)}, bf16[64,1024]{1,0:T(8,128)(2,1)S(1)}, u32[]{:S(2)}, u32[]{:S(2)}) collective-permute-start(bf16[64,1024]{1,0:T(8,128)(2,1)S(1)} %get-tuple-element.49), channel_id=1, source_target_pairs={{0,16},{1,17},{2,18},{3,19},{4,20},{5,21},{6,22},{7,23},{8,12},{9,... | collective-permute-start | bytes 393224 | tf_op jit(solution)/shard_map/ppermute | solution.py:267
  34.3 5.6 %collective-permute-start.18 = (bf16[64,1024]{1,0:T(8,128)(2,1)S(1)}, bf16[64,1024]{1,0:T(8,128)(2,1)S(1)}, u32[]{:S(2)}, u32[]{:S(2)}) collective-permute-start(bf16[64,1024]{1,0:T(8,128)(2,1)S(1)} %get-tuple-element.50), channel_id=1, source_target_pairs={{0,1},{1,0},{2,3},{3,2},{4,5},{5,4},{6,7},{7,6},{8,10},{9,11},{10,... | collective-permute-start | bytes 393224 | tf_op jit(solution)/shard_map/ppermute | solution.py:267
  36.0 6.2 %collective-permute-start.12 = (bf16[64,1024]{1,0:T(8,128)(2,1)S(1)}, bf16[64,1024]{1,0:T(8,128)(2,1)S(1)}, u32[]{:S(2)}, u32[]{:S(2)}) collective-permute-start(bf16[64,1024]{1,0:T(8,128)(2,1)S(1)} %get-tuple-element.42), channel_id=1, source_target_pairs={{0,17},{1,16},{2,19},{3,18},{4,21},{5,20},{6,23},{7,22},{8,14},{9,... | collective-permute-start | bytes 393224 | tf_op jit(solution)/shard_map/ppermute | solution.py:267
  38.3 5.2 %collective-permute-start.13 = (bf16[64,1024]{1,0:T(8,128)(2,1)S(1)}, bf16[64,1024]{1,0:T(8,128)(2,1)S(1)}, u32[]{:S(2)}, u32[]{:S(2)}) collective-permute-start(bf16[64,1024]{1,0:T(8,128)(2,1)S(1)} %get-tuple-element.43), channel_id=1, source_target_pairs={{0,16},{1,17},{2,18},{3,19},{4,20},{5,21},{6,22},{7,23},{8,12},{9,... | collective-permute-start | bytes 393224 | tf_op jit(solution)/shard_map/ppermute | solution.py:267
  38.3 5.6 %collective-permute-start.14 = (bf16[64,1024]{1,0:T(8,128)(2,1)S(1)}, bf16[64,1024]{1,0:T(8,128)(2,1)S(1)}, u32[]{:S(2)}, u32[]{:S(2)}) collective-permute-start(bf16[64,1024]{1,0:T(8,128)(2,1)S(1)} %get-tuple-element.44), channel_id=1, source_target_pairs={{0,1},{1,0},{2,3},{3,2},{4,5},{5,4},{6,7},{7,6},{8,10},{9,11},{10,... | collective-permute-start | bytes 393224 | tf_op jit(solution)/shard_map/ppermute | solution.py:267
  44.0 6.1 %collective-permute-start.19 = (bf16[16,2048]{1,0:T(8,128)(2,1)S(1)}, bf16[16,2048]{1,0:T(8,128)(2,1)S(1)}, u32[]{:S(2)}, u32[]{:S(2)}) collective-permute-start(bf16[16,2048]{1,0:T(8,128)(2,1)S(1)} %get-tuple-element.52), channel_id=1, source_target_pairs={{0,6},{1,7},{2,4},{3,5},{4,2},{5,3},{6,0},{7,1},{8,25},{9,24},{10,... | collective-permute-start | bytes 196616 | tf_op jit(solution)/shard_map/ppermute | solution.py:267
  44.1 6.1 %collective-permute-start.20 = (bf16[16,2048]{1,0:T(8,128)(2,1)S(1)}, bf16[16,2048]{1,0:T(8,128)(2,1)S(1)}, u32[]{:S(2)}, u32[]{:S(2)}) collective-permute-start(bf16[16,2048]{1,0:T(8,128)(2,1)S(1)} %get-tuple-element.53), channel_id=1, source_target_pairs={{0,4},{1,5},{2,6},{3,7},{4,0},{5,1},{6,2},{7,3},{8,24},{9,25},{10,... | collective-permute-start | bytes 196616 | tf_op jit(solution)/shard_map/ppermute | solution.py:267
  45.1 5.8 %collective-permute-start.21 = (bf16[16,2048]{1,0:T(8,128)(2,1)S(1)}, bf16[16,2048]{1,0:T(8,128)(2,1)S(1)}, u32[]{:S(2)}, u32[]{:S(2)}) collective-permute-start(bf16[16,2048]{1,0:T(8,128)(2,1)S(1)} %get-tuple-element.54), channel_id=1, source_target_pairs={{0,2},{1,3},{2,0},{3,1},{4,6},{5,7},{6,4},{7,5},{8,9},{9,8},{10,11... | collective-permute-start | bytes 196616 | tf_op jit(solution)/shard_map/ppermute | solution.py:267
